TPU v7x, 768 devices: a whole 4x8x12 slice. The times are simulated.
768 devices in a mesh: blk: 32 (over y_lo, x, core), grp: 24 (over y_hi, z).
Axes of the slice: x: 4, y: 8 (y_hi: 2, y_lo: 4; y = y_hi * 4 + y_lo), z: 12, core: 2. Of those that a mesh axis runs over, the one named last changes fastest.
Arguments:
- images: bfloat16 [18432, 1152], P('blk'), may hold values from -0.5 to 0.5, as said below
- texts: bfloat16 [18432, 1152], P(('blk', 'grp')), may hold values from -0.5 to 0.5
- log_scale: float32 [1], replicated, may hold values from 1.6 to 2.3
- bias: float32 [1], replicated, may hold values from -3 to -1
Outputs:
- d_images: float32 [18432, 1152], P(('blk', 'grp'))
- d_texts: float32 [18432, 1152], P(('blk', 'grp'))
Inputs may be any that keep to these rules, and one draw needn't show every extreme that they name: `images`: rows of image embeddings.
All inputs are finite; a program needn't handle non-finite values.
Results may differ from a plain program's by a relative error of at most 0.0051.
Values may be sent and summed in bfloat16 or wider, within the bound.
No kernel may reach another device: no remote copies, remote signals or barrier semaphores. Data moves between devices by JAX's collectives and lax.ppermute only.
A program may use at most 32 MiB of HBM per device.

v0:
```python
import jax
import jax.numpy as jnp
from jax import lax
from jax.sharding import PartitionSpec as P


def normalize(vectors):
    values = vectors.astype(jnp.float32)
    inverse = lax.rsqrt(jnp.sum(values * values, axis=1, keepdims=True) + 1e-06)
    return (values * inverse, inverse)


def unnormalize(unit_rows, inverse, grad_rows):
    inner = jnp.sum(unit_rows * grad_rows, axis=1, keepdims=True)
    return inverse * (grad_rows - unit_rows * inner)


def local(images, texts, log_scale, bias):
    groups = lax.axis_size("grp")
    blk_index = lax.axis_index("blk")
    grp_index = lax.axis_index("grp")
    text_rows = texts.shape[0]
    image_rows = images.shape[0]
    logit_scale = jnp.exp(log_scale[0])
    logit_shift = bias[0]
    unit_x, inv_x = normalize(images)
    unit_y, inv_y = normalize(texts)
    image_unit = unit_x.astype(jnp.bfloat16)
    text_unit = unit_y.astype(jnp.bfloat16)
    row_global = blk_index * image_rows + jnp.arange(image_rows, dtype=jnp.int32)
    gathered = lax.all_gather(text_unit, "blk", axis=0, tiled=True)
    columns = jnp.arange(gathered.shape[0], dtype=jnp.int32)
    col_global = (columns // text_rows * groups + grp_index) * text_rows + columns % text_rows
    logits = (
        jnp.dot(image_unit, gathered.T, preferred_element_type=jnp.float32) * logit_scale
        + logit_shift
    )
    positive = (row_global[:, None] == col_global[None, :]).astype(jnp.float32)
    weights = (jax.nn.sigmoid(logits) - positive).astype(jnp.bfloat16)
    image_term = jnp.dot(weights, gathered, preferred_element_type=jnp.float32)
    image_part = lax.psum_scatter(image_term * logit_scale, "grp", scatter_dimension=0, tiled=True)
    own_unit = lax.dynamic_slice_in_dim(unit_x, grp_index * text_rows, text_rows, 0)
    own_inverse = lax.dynamic_slice_in_dim(inv_x, grp_index * text_rows, text_rows, 0)
    d_images = unnormalize(own_unit, own_inverse, image_part)
    text_part = lax.psum_scatter(
        jnp.einsum("ic,ie->ce", weights, image_unit, preferred_element_type=jnp.float32)
        * logit_scale,
        "blk",
        scatter_dimension=0,
        tiled=True,
    )
    d_texts = unnormalize(unit_y, inv_y, text_part)
    return (d_images, d_texts)


def solution(mesh):
    return jax.shard_map(
        local,
        mesh=mesh,
        in_specs=(P("blk", None), P(("blk", "grp"), None), P(), P()),
        out_specs=(P(("blk", "grp"), None), P(("blk", "grp"), None)),
        check_vma=False,
    )
```

profile of v0, /device:TPU:64, one launch (start us, length us, event | category | flops | bytes accessed | tf_op | source)
XLA Modules:
  0.0 621.8 jit_solution(13736534469446873055)
XLA Ops:
  7.2 0.0 all-gather.2.cloned.1.call-start
  7.2 0.9 fusion.9
  8.2 1.5 fusion.5
  9.7 0.0 all-gather.2.cloned.1.call-update
  9.7 0.0 reduce-scatter.8.cloned.1.call-start
  11.1 1.7 fusion
  12.8 69.4 %all-gather.2.cloned.1.call-done = bf16[768,1152]{1,0:T(8,128)(2,1)} async-done(((bf16[24,1152]{1,0:T(8,128)(2,1)}), bf16[768,1152]{1,0:T(8,128)(2,1)}) %all-gather.2.cloned.1.call-update) | async-done | bytes 1769488 | tf_op jit(solution)/shard_map/all_gather | solution.py:31
  82.2 0.0 copy-start.2
  82.2 3.5 subtract_convert_fusion
  85.7 0.0 copy-done.2
  85.7 2.9 convolution_multiply_fusion.1
  88.6 0.0 copy-start
  88.6 0.0 reduce-scatter.8.cloned.1.call-update
  88.6 0.0 reduce-scatter.10.cloned.1.call-start
  88.6 1.2 copy-done
  89.9 3.5 convolution_multiply_fusion
  93.4 0.0 reduce-scatter.10.cloned.1.call-update
  93.4 0.1 dynamic-slice.3
  93.5 0.0 copy-start.1
  93.5 1.8 convert_multiply_fusion
  95.3 364.0 %reduce-scatter.8.cloned.1.call-done = f32[24,1152]{1,0:T(8,128)} async-done(((f32[576,1152]{1,0:T(8,128)}), f32[24,1152]{1,0:T(8,128)}) %reduce-scatter.8.cloned.1.call-update) | async-done | bytes 110608
  459.3 1.1 multiply_reduce_fusion
  460.4 1.7 subtract_multiply_fusion
  462.1 150.5 %reduce-scatter.10.cloned.1.call-done = f32[24,1152]{1,0:T(8,128)} async-done(((f32[768,1152]{1,0:T(8,128)}), f32[24,1152]{1,0:T(8,128)}) %reduce-scatter.10.cloned.1.call-update) | async-done | bytes 110608
  612.6 0.0 copy-done.1
  612.6 1.1 fusion.6
  613.7 1.6 fusion.8
  (4 shorter events, 0.0 us)
Async XLA Ops:
  7.2 75.0 %all-gather.2.cloned.1.call-start = ((), (), s32[]{:S(2)}) async-start(), calls=%async_computation.2 | async-start | bytes 1824768 | tf_op jit(solution)/shard_map/all_gather | solution.py:31
  9.7 449.6 %reduce-scatter.8.cloned.1.call-start = ((), (), s32[]{:S(2)}) async-start(), calls=%async_computation.3 | async-start | bytes 2764800
  82.2 3.5 copy-start.2
  88.6 1.3 copy-start
  88.6 524.0 %reduce-scatter.10.cloned.1.call-start = ((), (), s32[]{:S(2)}) async-start(), calls=%async_computation.4 | async-start | bytes 3649536
  93.5 519.1 %copy-start.1 = (bf16[24,1152]{1,0:T(8,128)(2,1)S(1)}, bf16[24,1152]{1,0:T(8,128)(2,1)}, u32[]{:S(2)}) copy-start(bf16[24,1152]{1,0:T(8,128)(2,1)} %param.5) | copy-start | bytes 165892
Sparse Core Ops, SparseCore 0:
  11.0 71.1 all-gather.1
  88.7 370.5 reduce-scatter.7
  462.5 150.0 reduce-scatter.9
where the time goes:
time: 622 us
  waiting for transfers between devices  584 us (94%)
  between operations  15.1 us (2%)
  other arithmetic  11.4 us (2%)
  matrix products  9.89 us (2%)
    unnamed x5, waiting for transfers between devices  515 us
    all_gather x1, waiting for transfers between devices, local(): gathered = lax.all_gather(text_unit, 'blk', axis=0, tiled=True)  69.4 us
  transfers between devices with their start and end apart: 3, of which 3 were waited for; matrix products, arithmetic and copies ran while one was open for 2% of the time, Pallas kernels for 0%

commit v1 on v0

v1 whole, which is shorter than its diff:
```python
import jax
import jax.numpy as jnp
from jax import lax
from jax.sharding import Mesh, PartitionSpec as P

SIZES = (4, 4, 2, 2, 3, 2, 2)
NAMES = ("yl", "x", "c", "yh", "z3", "z2", "z1")
ROWS = 24
BF = jnp.bfloat16
F32 = jnp.float32
TEXT_SIDE = "perm"
GATHER = "direct"


def normalize(vectors):
    values = vectors.astype(F32)
    inverse = lax.rsqrt(jnp.sum(values * values, axis=1, keepdims=True) + 1e-06)
    return values * inverse, inverse


def unnormalize(unit_rows, inverse, grad_rows):
    inner = jnp.sum(unit_rows * grad_rows, axis=1, keepdims=True)
    return inverse * (grad_rows - unit_rows * inner)


def pair_perm(size, distance):
    perm = []
    for core in range(2):
        for at in range(size):
            step = distance if (at // distance) % 2 == 0 else -distance
            if core:
                step = -step
            perm.append((core * size + at, core * size + (at + step) % size))
    return perm


def swap(value, axis):
    return lax.ppermute(value, axis, [(0, 1), (1, 0)])


def pick(value, axis, index):
    return lax.dynamic_index_in_dim(value, index, axis, keepdims=False)


def gather(texts):
    if GATHER == "direct":
        copies = jnp.broadcast_to(texts[None], (16, *texts.shape))
        own = lax.all_to_all(copies, ("yl", "x"), 0, 0).reshape(-1, texts.shape[1])
    else:
        copies = jnp.broadcast_to(texts[None], (4, *texts.shape))
        part = lax.all_to_all(copies, "yl", 0, 0).reshape(1, -1, texts.shape[1])
        part = jnp.broadcast_to(part, (4, *part.shape[1:]))
        own = lax.all_to_all(part, "x", 0, 0)
        own = own.reshape(4, 4, 24, -1).swapaxes(0, 1).reshape(-1, texts.shape[1])
    return own


def local(images, texts, log_scale, bias):
    width = texts.shape[1]
    scale = jnp.exp(log_scale[0])
    z1 = lax.axis_index("z1")
    group = lax.axis_index(("yh", "z3", "z2", "z1"))
    blocks = images.reshape(12, 2, ROWS, width)
    mine, theirs = pick(blocks, 1, z1), pick(blocks, 1, 1 - z1)
    image_rows = jnp.concatenate([theirs, mine], 0).reshape(-1, width)
    own = gather(texts)
    other = swap(own, "c")
    text_rows = jnp.concatenate([own, other], 0)
    xn = normalize(image_rows)[0].astype(BF)
    yn = normalize(text_rows)[0].astype(BF)
    logits = jnp.dot(xn, yn.T, preferred_element_type=F32) * scale + bias[0]
    w = jax.nn.sigmoid(logits).astype(BF)
    half = xn.shape[0] // 2
    gx_send = jnp.dot(w[:half], yn, preferred_element_type=F32).astype(BF)
    gx_got = lax.ppermute(gx_send, ("c", "z3", "z2", "z1"), pair_perm(12, 1))
    gy = jnp.einsum("ic,ie->ce", w, xn, preferred_element_type=F32)
    n_own = own.shape[0]
    gy_got = swap(gy[n_own:].astype(BF), "c")
    gx_keep = jnp.dot(w[half:], yn, preferred_element_type=F32)
    gx = (gx_keep + gx_got.astype(F32)).astype(BF).reshape(12, ROWS, width)
    gy = gy[:n_own] + gy_got.astype(F32)
    gx = lax.all_to_all(gx, ("yh", "z3", "z2"), 0, 0)
    if TEXT_SIDE == "a2a":
        gy = gy.astype(BF).reshape(16, ROWS, width)
        gy = lax.all_to_all(gy, ("yl", "x"), 0, 0)
        gy = jnp.sum(gy.astype(F32), 0)
    else:
        x, yl = lax.axis_index("x"), lax.axis_index("yl")
        gy = gy.reshape(2, 2, 2, 2, ROWS, width)
        def stage(gy, axis, bit, move):
            keep = pick(gy, axis, bit)
            send = pick(gy, axis, 1 - bit).astype(BF)
            return keep + move(send).astype(F32)
        flip = lambda n, d: [(i, i ^ d) for i in range(n)]
        gy = stage(gy, 3, x % 2, lambda v: lax.ppermute(v, ("x", "c"), [((i * 2 + c), ((i + (1 if (i + c) % 2 == 0 else -1)) % 4) * 2 + c) for i in range(4) for c in range(2)]))
        gy = stage(gy, 2, x // 2, lambda v: lax.ppermute(v, "x", flip(4, 2)))
        gy = stage(gy, 1, yl % 2, lambda v: lax.ppermute(v, "yl", flip(4, 1)))
        gy = stage(gy, 0, yl // 2, lambda v: lax.ppermute(v, "yl", flip(4, 2)))
    gx = jnp.sum(gx.astype(F32), 0)
    own_images = lax.dynamic_slice_in_dim(images, group * ROWS, ROWS, 0)
    unit_x, inv_x = normalize(own_images)
    unit_y, inv_y = normalize(texts)
    gx = (gx - unit_y.astype(BF).astype(F32)) * scale
    gy = (gy - unit_x.astype(BF).astype(F32)) * scale
    return unnormalize(unit_x, inv_x, gx), unnormalize(unit_y, inv_y, gy)


def solution(mesh):
    fine = Mesh(mesh.devices.reshape(SIZES), NAMES)
    blk, grp = NAMES[:3], NAMES[3:]
    return jax.shard_map(
        local,
        mesh=fine,
        in_specs=(P(blk, None), P(blk + grp, None), P(), P()),
        out_specs=(P(blk + grp, None), P(blk + grp, None)),
        check_vma=False,
    )
```

time: 622 us -> 124 us (0.20)
  the two profiles are of different devices: /device:TPU:64 before, /device:TPU:108 now
where the time goes in v1:
time: 124 us; the launch traced here: 123 us
  waiting for transfers between devices  59 us (48%)
  starting transfers between devices  40.9 us (33%)
  other arithmetic  8.29 us (7%)
  matrix products  7.98 us (6%)
  local copies, waits for them, and re-layouts  4.87 us (4%)
  between operations  2.35 us (2%)
    ppermute x1, waiting for transfers between devices, local(): gy = stage(gy, 1, yl % 2, lambda v: lax.ppermute(v, 'yl', flip(4, 1)))  21.4 us
    all_to_all x1, waiting for transfers between devices, gather(): own = lax.all_to_all(copies, ('yl', 'x'), 0, 0).reshape(-1, texts.shape[1])  19.5 us
    all_to_all x1, starting transfers between devices, local(): gx = lax.all_to_all(gx, ('yh', 'z3', 'z2'), 0, 0)  19 us
    ppermute x1, waiting for transfers between devices, local(): gy = stage(gy, 2, x // 2, lambda v: lax.ppermute(v, 'x', flip(4, 2)))  7.22 us
    all_to_all x1, starting transfers between devices, gather(): own = lax.all_to_all(copies, ('yl', 'x'), 0, 0).reshape(-1, texts.shape[1])  5.95 us
    ppermute x1, waiting for transfers between devices, local(): gy = stage(gy, 0, yl // 2, lambda v: lax.ppermute(v, 'yl', flip(4, 2)))  4.91 us
    ppermute x1, waiting for transfers between devices, local(): gx_got = lax.ppermute(gx_send, ('c', 'z3', 'z2', 'z1'), pair_perm(12, 1))  4.03 us
    ppermute x2, starting transfers between devices, swap(): return lax.ppermute(value, axis, [(0, 1), (1, 0)])  3.94 us
  transfers between devices with their start and end apart: 9, of which 6 were waited for; matrix products, arithmetic and copies ran while one was open for 9% of the time, Pallas kernels for 0%

profile of v1, /device:TPU:108, one launch (start us, length us, event | category | flops | bytes accessed | tf_op | source)
XLA Modules:
  0.0 123.4 jit_solution(12070176247652597216)
XLA Ops:
  0.6 0.0 copy-start.2
  0.6 1.9 %broadcast_in_dim.2 = bf16[16,24,1152]{2,1,0:T(8,128)(2,1)} broadcast(bf16[24,1152]{1,0:T(8,128)(2,1)} %param.5), dimensions={1,2} | broadcast | bytes 940032 | tf_op jit(solution)/shard_map/broadcast_in_dim | solution.py:47
  2.5 5.9 %all-to-all-start = ((bf16[16,24,1152]{2,1,0:T(8,128)(2,1)}), bf16[16,24,1152]{2,1,0:T(8,128)(2,1)S(1)}, u32[]{:S(2)}, u32[]{:S(2)}) async-start(bf16[16,24,1152]{2,1,0:T(8,128)(2,1)} %broadcast_in_dim.2), calls=%async_computation | async-start | bytes 1769472 | tf_op jit(solution)/shard_map/all_to_all | solution.py:48
  8.5 0.0 copy-done.2
  8.5 0.1 dynamic-slice_bitcast_fusion.1
  8.6 0.3 multiply_reduce_fusion
  9.0 0.1 rsqrt.37
  10.4 19.5 %all-to-all-done = bf16[16,24,1152]{2,1,0:T(8,128)(2,1)S(1)} async-done(((bf16[16,24,1152]{2,1,0:T(8,128)(2,1)}), bf16[16,24,1152]{2,1,0:T(8,128)(2,1)S(1)}, u32[]{:S(2)}, u32[]{:S(2)}) %all-to-all-start) | async-done | bytes 884768 | tf_op jit(solution)/shard_map/all_to_all | solution.py:48
  29.9 1.9 %collective-permute-start = (bf16[384,1152]{1,0:T(8,128)(2,1)S(1)}, bf16[384,1152]{1,0:T(8,128)(2,1)S(1)}, u32[]{:S(2)}, u32[]{:S(2)}) collective-permute-start(bf16[384,1152]{1,0:T(8,128)(2,1)S(1)} %bitcast.44), channel_id=1, source_target_pairs={{0,24},{24,0},{1,25},{25,1},{2,26},{26,2},{3,27},{27,3},{4,28},{28... | collective-permute-start | bytes 2654216 | tf_op jit(solution)/shard_map/ppermute | solution.py:38
  31.8 0.2 maximum_convert_fusion
  32.0 0.2 fusion.2
  32.2 2.0 %collective-permute-done = bf16[384,1152]{1,0:T(8,128)(2,1)S(1)} collective-permute-done((bf16[384,1152]{1,0:T(8,128)(2,1)S(1)}, bf16[384,1152]{1,0:T(8,128)(2,1)S(1)}, u32[]{:S(2)}, u32[]{:S(2)}) %collective-permute-start) | collective-permute-done | bytes 884768 | tf_op jit(solution)/shard_map/ppermute | solution.py:38
  34.2 0.4 fusion
  34.6 1.6 %divide_convert_fusion = bf16[576,768]{1,0:T(8,128)(2,1)S(1)} fusion(bf16[576,1152]{1,0:T(8,128)(2,1)S(1)} %fusion.2, f32[]{:T(128)} %bitcast.41, f32[]{:T(128)} %bitcast.5, f32[768]{0:T(1024)S(1)} %add_rsqrt_fusion.1, bf16[384,1152]{1,0:T(8,128)(2,1)S(1)} %collective-permute-done, bf16[384,1152]{1,0:T(8,128)(2,1)S(1)} %bitcast.46), kind=kOutput, calls=%fused_computation.11 | convolution fusion | flops 1027178496 | bytes 3984392 | tf_op jit(solution)/shard_map/dot_general | solution.py:71
  36.3 0.0 copy-start.4
  36.3 1.7 %fusion.31 = f32[768,1152]{1,0:T(8,128)S(1)} fusion(bf16[576,768]{1,0:T(8,128)(2,1)S(1)} %divide_convert_fusion, bf16[576,1152]{1,0:T(8,128)(2,1)S(1)} %fusion.2), kind=kOutput, calls=%fused_computation.59 | convolution fusion | flops 1019215872 | bytes 5750784 | tf_op jit(solution)/shard_map/ic,ie->ce/dot_general | solution.py:76
  38.0 0.0 copy-start
  38.0 1.7 %copy-done = f32[768,1152]{1,0:T(8,128)} copy-done((f32[768,1152]{1,0:T(8,128)}, f32[768,1152]{1,0:T(8,128)S(1)}, u32[]{:S(2)}) %copy-start) | copy-done | bytes 3538968
  39.8 0.1 slice.29
  39.9 2.0 %collective-permute-start.2 = (bf16[384,1152]{1,0:T(8,128)(2,1)S(1)}, bf16[384,1152]{1,0:T(8,128)(2,1)}, u32[]{:S(2)}, u32[]{:S(2)}) collective-permute-start(bf16[384,1152]{1,0:T(8,128)(2,1)S(1)} %slice.29), channel_id=1, source_target_pairs={{0,24},{24,0},{1,25},{25,1},{2,26},{26,2},{3,27},{27,3},{4,28},{28... | collective-permute-start | bytes 2654216 | tf_op jit(solution)/shard_map/ppermute | solution.py:38
  41.9 0.0 copy-start.1
  41.9 1.7 %convolution_convert_fusion = bf16[288,1152]{1,0:T(8,128)(2,1)} fusion(bf16[576,768]{1,0:T(8,128)(2,1)S(1)} %divide_convert_fusion, f32[768]{0:T(1024)S(1)} %add_rsqrt_fusion.1, bf16[384,1152]{1,0:T(8,128)(2,1)S(1)} %collective-permute-done, bf16[384,1152]{1,0:T(8,128)(2,1)S(1)} %bitcast.47), kind=kOutput, calls=%fused_computation.7 | convolution fusion | flops 515248128 | bytes 2879488 | tf_op jit(solution)/shard_map/dot_general | solution.py:74
  43.7 0.0 copy-done.4
  43.7 1.9 %collective-permute-start.1 = (bf16[288,1152]{1,0:T(8,128)(2,1)}, bf16[288,1152]{1,0:T(8,128)(2,1)}, u32[]{:S(2)}, u32[]{:S(2)}) collective-permute-start(bf16[288,1152]{1,0:T(8,128)(2,1)} %convolution_convert_fusion), channel_id=1, source_target_pairs={{0,1},{1,0},{2,3},{3,2},{4,5},{5,4},{6,7},{7,6},{8,9},{9,8},{10,11... | collective-permute-start | bytes 1990664 | tf_op jit(solution)/shard_map/ppermute | solution.py:75
  45.6 0.0 collective-permute-done.2
  45.6 0.0 copy-done.1
  45.6 1.4 %slice_add_fusion = f32[384,1152]{1,0:T(8,128)S(1)} fusion(f32[768,1152]{1,0:T(8,128)S(1)} %copy-done.1, bf16[384,1152]{1,0:T(8,128)(2,1)} %collective-permute-done.2), kind=kLoop, calls=%fused_computation.9 | loop fusion | flops 884736 | bytes 4423680 | tf_op jit(solution)/shard_map/add | solution.py:81
  47.0 0.8 fusion.3
  47.8 2.8 %collective-permute-start.3 = (bf16[2,2,2,24,1152]{4,3,0,1,2:T(8,128)(2,1)}, bf16[2,2,2,24,1152]{4,3,0,1,2:T(8,128)(2,1)}, u32[]{:S(2)}, u32[]{:S(2)}) collective-permute-start(bf16[2,2,2,24,1152]{4,3,0,1,2:T(8,128)(2,1)} %fusion.3), channel_id=1, source_target_pairs={{0,48},{24,168},{48,0},{72,120},{96,144},{120,72},{144,96},{168,24... | collective-permute-start | bytes 1327112 | tf_op jit(solution)/shard_map/ppermute | solution.py:95
  50.6 0.9 fusion.19
  51.6 0.9 fusion.23
  52.5 4.0 %collective-permute-done.1 = bf16[288,1152]{1,0:T(8,128)(2,1)} collective-permute-done((bf16[288,1152]{1,0:T(8,128)(2,1)}, bf16[288,1152]{1,0:T(8,128)(2,1)}, u32[]{:S(2)}, u32[]{:S(2)}) %collective-permute-start.1) | collective-permute-done | bytes 663584 | tf_op jit(solution)/shard_map/ppermute | solution.py:75
  56.5 2.9 %add_convert_fusion = bf16[288,1152]{1,0:T(8,128)(2,1)} fusion(bf16[288,1152]{1,0:T(8,128)(2,1)} %collective-permute-done.1, bf16[576,768]{1,0:T(8,128)(2,1)} %copy-done.4, f32[768]{0:T(1024)S(1)} %add_rsqrt_fusion.1, bf16[384,1152]{1,0:T(8,128)(2,1)S(1)} %collective-permute-done, bf16[384,1152]{1,0:T(8,128)(2,1)S(1)} %bitcast.48), kind=kOutput, calls=%fused_computation.14 | convolution fusion | flops 515911680 | bytes 3542016 | tf_op jit(solution)/shard_map/dot_general | solution.py:79
  59.4 19.0 %all-to-all-start.1 = ((bf16[12,24,1152]{2,1,0:T(8,128)(2,1)}), bf16[12,24,1152]{2,1,0:T(8,128)(2,1)S(1)}, u32[]{:S(2)}, u32[]{:S(2)}) async-start(bf16[12,24,1152]{2,1,0:T(8,128)(2,1)} %bitcast.50), calls=%async_computation.1 | async-start | bytes 1327104 | tf_op jit(solution)/shard_map/all_to_all | solution.py:82
  78.4 0.0 collective-permute-done.3
  78.4 1.1 bitcast_add_fusion
  79.5 0.0 copy-start.3
  79.6 3.4 %collective-permute-start.4 = (bf16[2,2,24,1152]{3,2,0,1:T(8,128)(2,1)S(1)}, bf16[2,2,24,1152]{3,2,0,1:T(8,128)(2,1)S(1)}, u32[]{:S(2)}, u32[]{:S(2)}) collective-permute-start(bf16[2,2,24,1152]{3,2,0,1:T(8,128)(2,1)S(1)} %fusion.9), channel_id=1, source_target_pairs={{0,96},{48,144},{96,0},{144,48},{1,97},{49,145},{97,1},{145,49},{2... | collective-permute-start | bytes 663560 | tf_op jit(solution)/shard_map/ppermute | solution.py:96
  83.0 7.2 %collective-permute-done.4 = bf16[2,2,24,1152]{3,2,0,1:T(8,128)(2,1)S(1)} collective-permute-done((bf16[2,2,24,1152]{3,2,0,1:T(8,128)(2,1)S(1)}, bf16[2,2,24,1152]{3,2,0,1:T(8,128)(2,1)S(1)}, u32[]{:S(2)}, u32[]{:S(2)}) %collective-permute-start.4) | collective-permute-done | bytes 221216 | tf_op jit(solution)/shard_map/ppermute | solution.py:96
  90.3 2.1 %collective-permute-start.5 = (bf16[2,24,1152]{2,1,0:T(8,128)(2,1)S(1)}, bf16[2,24,1152]{2,1,0:T(8,128)(2,1)S(1)}, u32[]{:S(2)}, u32[]{:S(2)}) collective-permute-start(bf16[2,24,1152]{2,1,0:T(8,128)(2,1)S(1)} %fusion.24), channel_id=1, source_target_pairs={{0,192},{192,0},{384,576},{576,384},{1,193},{193,1},{385,577},{577... | collective-permute-start | bytes 331784 | tf_op jit(solution)/shard_map/ppermute | solution.py:97
  92.4 21.4 %collective-permute-done.5 = bf16[2,24,1152]{2,1,0:T(8,128)(2,1)S(1)} collective-permute-done((bf16[2,24,1152]{2,1,0:T(8,128)(2,1)S(1)}, bf16[2,24,1152]{2,1,0:T(8,128)(2,1)S(1)}, u32[]{:S(2)}, u32[]{:S(2)}) %collective-permute-start.5) | collective-permute-done | bytes 110624 | tf_op jit(solution)/shard_map/ppermute | solution.py:97
  113.8 1.9 %collective-permute-start.6 = (bf16[24,1152]{1,0:T(8,128)(2,1)S(1)}, bf16[24,1152]{1,0:T(8,128)(2,1)S(1)}, u32[]{:S(2)}, u32[]{:S(2)}) collective-permute-start(bf16[24,1152]{1,0:T(8,128)(2,1)S(1)} %fusion.27), channel_id=1, source_target_pairs={{0,384},{192,576},{384,0},{576,192},{1,385},{193,577},{385,1},{577... | collective-permute-start | bytes 165896 | tf_op jit(solution)/shard_map/ppermute | solution.py:98
  115.7 0.0 all-to-all-done.1
  115.7 0.1 convert_reduce_fusion
  115.8 4.9 %collective-permute-done.6 = bf16[24,1152]{1,0:T(8,128)(2,1)S(1)} collective-permute-done((bf16[24,1152]{1,0:T(8,128)(2,1)S(1)}, bf16[24,1152]{1,0:T(8,128)(2,1)S(1)}, u32[]{:S(2)}, u32[]{:S(2)}) %collective-permute-start.6) | collective-permute-done | bytes 55328 | tf_op jit(solution)/shard_map/ppermute | solution.py:98
  120.7 0.0 copy-done.3
  120.7 1.0 fusion.20
  121.8 1.6 %fusion.22 = (f32[24,1152]{1,0:T(8,128)}, f32[24,1152]{1,0:T(8,128)}) fusion(bf16[24,1152]{1,0:T(8,128)(2,1)S(1)} %copy-done.3, f32[24]{0:T(128)S(1)} %get-tuple-element.2, f32[24]{0:T(128)S(1)} %add_rsqrt_fusion.2, f32[]{:T(128)} %bitcast.5, f32[24]{0:T(128)S(1)} %add_rsqrt_fusion.3, bf16[576,1152]{1,0:T(8,128)(2,1)} %param.4, s32[]{:T(128)S(6)} %select_n.56, ...), kind=kLoop, calls=%fused_computation.44 | loop fusion | flops 552960 | bytes 608652 | tf_op jit(solution)/shard_map/mul | solution.py:23
  (9 shorter events, 0.2 us)
Async XLA Ops:
  0.6 7.9 %copy-start.2 = (bf16[576,1152]{1,0:T(8,128)(2,1)S(1)}, bf16[576,1152]{1,0:T(8,128)(2,1)}, u32[]{:S(2)}) copy-start(bf16[576,1152]{1,0:T(8,128)(2,1)} %param.4) | copy-start | bytes 3981316
  2.5 27.4 %all-to-all-start = ((bf16[16,24,1152]{2,1,0:T(8,128)(2,1)}), bf16[16,24,1152]{2,1,0:T(8,128)(2,1)S(1)}, u32[]{:S(2)}, u32[]{:S(2)}) async-start(bf16[16,24,1152]{2,1,0:T(8,128)(2,1)} %broadcast_in_dim.2), calls=%async_computation | async-start | bytes 1769472 | tf_op jit(solution)/shard_map/all_to_all | solution.py:48
  29.9 4.3 %collective-permute-start = (bf16[384,1152]{1,0:T(8,128)(2,1)S(1)}, bf16[384,1152]{1,0:T(8,128)(2,1)S(1)}, u32[]{:S(2)}, u32[]{:S(2)}) collective-permute-start(bf16[384,1152]{1,0:T(8,128)(2,1)S(1)} %bitcast.44), channel_id=1, source_target_pairs={{0,24},{24,0},{1,25},{25,1},{2,26},{26,2},{3,27},{27,3},{4,28},{28... | collective-permute-start | bytes 2654216 | tf_op jit(solution)/shard_map/ppermute | solution.py:38
  36.3 7.4 %copy-start.4 = (bf16[576,768]{1,0:T(8,128)(2,1)}, bf16[576,768]{1,0:T(8,128)(2,1)S(1)}, u32[]{:S(2)}) copy-start(bf16[576,768]{1,0:T(8,128)(2,1)S(1)} %divide_convert_fusion) | copy-start | bytes 2654212
  38.0 1.8 %copy-start = (f32[768,1152]{1,0:T(8,128)}, f32[768,1152]{1,0:T(8,128)S(1)}, u32[]{:S(2)}) copy-start(f32[768,1152]{1,0:T(8,128)S(1)} %fusion.31) | copy-start | bytes 10616836
  39.9 5.7 %collective-permute-start.2 = (bf16[384,1152]{1,0:T(8,128)(2,1)S(1)}, bf16[384,1152]{1,0:T(8,128)(2,1)}, u32[]{:S(2)}, u32[]{:S(2)}) collective-permute-start(bf16[384,1152]{1,0:T(8,128)(2,1)S(1)} %slice.29), channel_id=1, source_target_pairs={{0,24},{24,0},{1,25},{25,1},{2,26},{26,2},{3,27},{27,3},{4,28},{28... | collective-permute-start | bytes 2654216 | tf_op jit(solution)/shard_map/ppermute | solution.py:38
  41.9 3.7 %copy-start.1 = (f32[768,1152]{1,0:T(8,128)S(1)}, f32[768,1152]{1,0:T(8,128)}, u32[]{:S(2)}) copy-start(f32[768,1152]{1,0:T(8,128)} %copy-done) | copy-start | bytes 10616836
  43.7 12.9 %collective-permute-start.1 = (bf16[288,1152]{1,0:T(8,128)(2,1)}, bf16[288,1152]{1,0:T(8,128)(2,1)}, u32[]{:S(2)}, u32[]{:S(2)}) collective-permute-start(bf16[288,1152]{1,0:T(8,128)(2,1)} %convolution_convert_fusion), channel_id=1, source_target_pairs={{0,1},{1,0},{2,3},{3,2},{4,5},{5,4},{6,7},{7,6},{8,9},{9,8},{10,11... | collective-permute-start | bytes 1990664 | tf_op jit(solution)/shard_map/ppermute | solution.py:75
  47.8 30.7 %collective-permute-start.3 = (bf16[2,2,2,24,1152]{4,3,0,1,2:T(8,128)(2,1)}, bf16[2,2,2,24,1152]{4,3,0,1,2:T(8,128)(2,1)}, u32[]{:S(2)}, u32[]{:S(2)}) collective-permute-start(bf16[2,2,2,24,1152]{4,3,0,1,2:T(8,128)(2,1)} %fusion.3), channel_id=1, source_target_pairs={{0,48},{24,168},{48,0},{72,120},{96,144},{120,72},{144,96},{168,24... | collective-permute-start | bytes 1327112 | tf_op jit(solution)/shard_map/ppermute | solution.py:95
  59.4 56.3 %all-to-all-start.1 = ((bf16[12,24,1152]{2,1,0:T(8,128)(2,1)}), bf16[12,24,1152]{2,1,0:T(8,128)(2,1)S(1)}, u32[]{:S(2)}, u32[]{:S(2)}) async-start(bf16[12,24,1152]{2,1,0:T(8,128)(2,1)} %bitcast.50), calls=%async_computation.1 | async-start | bytes 1327104 | tf_op jit(solution)/shard_map/all_to_all | solution.py:82
  79.5 41.2 %copy-start.3 = (bf16[24,1152]{1,0:T(8,128)(2,1)S(1)}, bf16[24,1152]{1,0:T(8,128)(2,1)}, u32[]{:S(2)}) copy-start(bf16[24,1152]{1,0:T(8,128)(2,1)} %param.5) | copy-start | bytes 165892
  79.6 10.6 %collective-permute-start.4 = (bf16[2,2,24,1152]{3,2,0,1:T(8,128)(2,1)S(1)}, bf16[2,2,24,1152]{3,2,0,1:T(8,128)(2,1)S(1)}, u32[]{:S(2)}, u32[]{:S(2)}) collective-permute-start(bf16[2,2,24,1152]{3,2,0,1:T(8,128)(2,1)S(1)} %fusion.9), channel_id=1, source_target_pairs={{0,96},{48,144},{96,0},{144,48},{1,97},{49,145},{97,1},{145,49},{2... | collective-permute-start | bytes 663560 | tf_op jit(solution)/shard_map/ppermute | solution.py:96
  90.3 23.5 %collective-permute-start.5 = (bf16[2,24,1152]{2,1,0:T(8,128)(2,1)S(1)}, bf16[2,24,1152]{2,1,0:T(8,128)(2,1)S(1)}, u32[]{:S(2)}, u32[]{:S(2)}) collective-permute-start(bf16[2,24,1152]{2,1,0:T(8,128)(2,1)S(1)} %fusion.24), channel_id=1, source_target_pairs={{0,192},{192,0},{384,576},{576,384},{1,193},{193,1},{385,577},{577... | collective-permute-start | bytes 331784 | tf_op jit(solution)/shard_map/ppermute | solution.py:97
  113.8 6.9 %collective-permute-start.6 = (bf16[24,1152]{1,0:T(8,128)(2,1)S(1)}, bf16[24,1152]{1,0:T(8,128)(2,1)S(1)}, u32[]{:S(2)}, u32[]{:S(2)}) collective-permute-start(bf16[24,1152]{1,0:T(8,128)(2,1)S(1)} %fusion.27), channel_id=1, source_target_pairs={{0,384},{192,576},{384,0},{576,192},{1,385},{193,577},{385,1},{577... | collective-permute-start | bytes 165896 | tf_op jit(solution)/shard_map/ppermute | solution.py:98

commit v2 on v1

v2 whole, which is shorter than its diff:
```python
import jax
import jax.numpy as jnp
from jax import lax
from jax.sharding import Mesh, PartitionSpec as P

SIZES = (4, 4, 2, 2, 3, 2, 2)
NAMES = ("yl", "x", "c", "yh", "z3", "z2", "z1")
ROWS = 24
BF = jnp.bfloat16
F32 = jnp.float32


def normalize(vectors):
    values = vectors.astype(F32)
    inverse = lax.rsqrt(jnp.sum(values * values, axis=1, keepdims=True) + 1e-06)
    return values * inverse, inverse


def unnormalize(unit_rows, inverse, grad_rows):
    inner = jnp.sum(unit_rows * grad_rows, axis=1, keepdims=True)
    return inverse * (grad_rows - unit_rows * inner)


def pair_perm(size, distance):
    perm = []
    for core in range(2):
        for at in range(size):
            step = distance if (at // distance) % 2 == 0 else -distance
            if core:
                step = -step
            perm.append((core * size + at, core * size + (at + step) % size))
    return perm


def flip(value, axis, distance):
    size = lax.axis_size(axis)
    return lax.ppermute(value, axis, [(i, i ^ distance) for i in range(size)])


def pick(value, axis, index):
    return lax.dynamic_index_in_dim(value, index, axis, keepdims=False)


PLANE = ("yl", "x", "c", "yh")


def member(core, window, pos, x):
    y = (4 * window + pos - 2 * core) % 8
    return ((y % 4 * 4 + x) * 2 + core) * 2 + y // 4


PLACES = [(c, w, p, x) for c in range(2) for w in range(2) for p in range(4) for x in range(4)]


def gather(texts):
    groups = [
        [member(c, w, p, x) for x in range(4) for p in range(4)] for c in range(2) for w in range(2)
    ]
    copies = jnp.broadcast_to(texts[None], (16, *texts.shape))
    own = lax.all_to_all(copies, PLANE, 0, 0, axis_index_groups=groups)
    return own.reshape(-1, texts.shape[1])


def scatter_sum(total):
    pos = (lax.axis_index("yl") + 2 * lax.axis_index("c")) % 4
    for at, dp, dx in ((lax.axis_index("x"), 0, 1), (pos, 1, 0)):
        got = [
            lax.ppermute(
                pick(total, 0, at ^ d).astype(BF),
                PLANE,
                [(member(*m), member(m[0], m[1], m[2] ^ d * dp, m[3] ^ d * dx)) for m in PLACES],
            )
            for d in (1, 2, 3)
        ]
        total = pick(total, 0, at) + got[0].astype(F32) + got[1].astype(F32) + got[2].astype(F32)
    return total


def local(images, texts, log_scale, bias):
    width = texts.shape[1]
    scale = jnp.exp(log_scale[0])
    z1 = lax.axis_index("z1")
    group = lax.axis_index(("yh", "z3", "z2", "z1"))
    blocks = images.reshape(6, 2, 2, ROWS, width)
    mine, theirs = (pick(blocks, 2, i).swapaxes(0, 1).reshape(12, ROWS, width) for i in (z1, 1 - z1))
    image_rows = jnp.concatenate([theirs, mine], 0).reshape(-1, width)
    own = gather(texts)
    other = flip(own, "c", 1)
    text_rows = jnp.concatenate([own, other], 0)
    xn = normalize(image_rows)[0].astype(BF)
    yn = normalize(text_rows)[0].astype(BF)
    logits = jnp.dot(xn, yn.T, preferred_element_type=F32) * scale + bias[0]
    w = jax.nn.sigmoid(logits).astype(BF)
    half = xn.shape[0] // 2
    n_own = own.shape[0]
    gx_send = jnp.dot(w[:half], yn, preferred_element_type=F32).astype(BF)
    w, gx_send = lax.optimization_barrier((w, gx_send))
    gx_got = lax.ppermute(gx_send, ("c", "z3", "z2", "z1"), pair_perm(12, 1))
    gy_other = jnp.einsum("ic,ie->ce", w[:, n_own:], xn, preferred_element_type=F32).astype(BF)
    gy_own = jnp.einsum("ic,ie->ce", w[:, :n_own], xn, preferred_element_type=F32)
    gy_got = flip(gy_other, "c", 1)
    gx_keep = jnp.dot(w[half:], yn, preferred_element_type=F32)
    gx_got, gx_keep = lax.optimization_barrier((gx_got, gx_keep))
    z2 = lax.axis_index("z2")
    gx = (gx_keep + gx_got.astype(F32)).reshape(2, 6, ROWS, width)
    gx_got = lax.ppermute(pick(gx, 0, 1 - z2).astype(BF), ("c", "z3", "z2", "z1"), pair_perm(12, 2))
    gx = (pick(gx, 0, z2) + gx_got.astype(F32)).astype(BF)
    gx = lax.all_to_all(gx, ("yh", "z3"), 0, 0)
    gy = (gy_own + gy_got.astype(F32)).reshape(4, 4, ROWS, width)
    gy = scatter_sum(gy)
    gx = jnp.sum(gx.astype(F32), 0)
    own_images = lax.dynamic_slice_in_dim(images, group * ROWS, ROWS, 0)
    unit_x, inv_x = normalize(own_images)
    unit_y, inv_y = normalize(texts)
    gx = (gx - unit_y.astype(BF).astype(F32)) * scale
    gy = (gy - unit_x.astype(BF).astype(F32)) * scale
    return unnormalize(unit_x, inv_x, gx), unnormalize(unit_y, inv_y, gy)


def solution(mesh):
    fine = Mesh(mesh.devices.reshape(SIZES), NAMES)
    blk, grp = NAMES[:3], NAMES[3:]
    return jax.shard_map(
        local,
        mesh=fine,
        in_specs=(P(blk, None), P(blk + grp, None), P(), P()),
        out_specs=(P(blk + grp, None), P(blk + grp, None)),
        check_vma=False,
    )
```

time: 124 us -> 105 us (0.85)
  the two profiles are of different devices: /device:TPU:108 before, /device:TPU:64 now
where the time goes in v2:
time: 105 us; the launch traced here: 104 us
  starting transfers between devices  57.2 us (54%)
  waiting for transfers between devices  27.4 us (26%)
  matrix products  7.19 us (7%)
  other arithmetic  7.04 us (7%)
  local copies, waits for them, and re-layouts  2.45 us (2%)
  between operations  2.42 us (2%)
    ppermute x6, starting transfers between devices, scatter_sum(): lax.ppermute(pick(total, 0, at ^ d).astype(BF), PLANE, [(member(*m), memb...  20.7 us
    all_to_all x1, starting transfers between devices, local(): gx = lax.all_to_all(gx, ('yh', 'z3'), 0, 0)  14.7 us
    all_to_all x1, waiting for transfers between devices, gather(): own = lax.all_to_all(copies, PLANE, 0, 0, axis_index_groups=groups)  13.3 us
    all_to_all x1, waiting for transfers between devices, local(): gx = lax.all_to_all(gx, ('yh', 'z3'), 0, 0)  8.56 us
    all_to_all x1, starting transfers between devices, gather(): own = lax.all_to_all(copies, PLANE, 0, 0, axis_index_groups=groups)  7.44 us
    ppermute x1, starting transfers between devices, local(): gx_got = lax.ppermute(gx_send, ('c', 'z3', 'z2', 'z1'), pair_perm(12, 1))  5.21 us
    ppermute x1, starting transfers between devices, local(): lax.ppermute(pick(gx, 0, 1 - z2).astype(BF), ('c', 'z3', 'z2', 'z1'), pai...  4.79 us
    ppermute x2, starting transfers between devices, flip(): return lax.ppermute(value, axis, [(i, i ^ distance) for i in range(size)])  4.35 us
  transfers between devices with their start and end apart: 12, of which 4 were waited for; matrix products, arithmetic and copies ran while one was open for 8% of the time, Pallas kernels for 0%

profile of v2, /device:TPU:64, one launch (start us, length us, event | category | flops | bytes accessed | tf_op | source)
XLA Modules:
  0.0 103.7 jit_solution(4047527950731721533)
XLA Ops:
  0.6 0.0 copy-start
  0.6 1.9 %broadcast_in_dim.2 = bf16[16,24,1152]{2,1,0:T(8,128)(2,1)} broadcast(bf16[24,1152]{1,0:T(8,128)(2,1)} %param.5), dimensions={1,2} | broadcast | bytes 940032 | tf_op jit(solution)/shard_map/broadcast_in_dim | solution.py:59
  2.5 7.4 %all-to-all-start = ((bf16[16,24,1152]{2,1,0:T(8,128)(2,1)}), bf16[16,24,1152]{2,1,0:T(8,128)(2,1)S(1)}, u32[]{:S(2)}, u32[]{:S(2)}) async-start(bf16[16,24,1152]{2,1,0:T(8,128)(2,1)} %broadcast_in_dim.2), calls=%async_computation | async-start | bytes 1769472 | tf_op jit(solution)/shard_map/all_to_all | solution.py:60
  10.7 0.0 copy-done
  10.7 0.2 constant_dynamic-slice_fusion.1
  10.9 0.1 copy.11
  10.9 0.1 copy.10
  11.0 0.3 multiply_reduce_fusion
  11.3 0.1 rsqrt.37
  12.1 0.9 fusion.31
  13.0 13.3 %all-to-all-done = bf16[16,24,1152]{2,1,0:T(8,128)(2,1)S(1)} async-done(((bf16[16,24,1152]{2,1,0:T(8,128)(2,1)}), bf16[16,24,1152]{2,1,0:T(8,128)(2,1)S(1)}, u32[]{:S(2)}, u32[]{:S(2)}) %all-to-all-start) | async-done | bytes 884768 | tf_op jit(solution)/shard_map/all_to_all | solution.py:60
  26.3 2.4 %collective-permute-start = (bf16[384,1152]{1,0:T(8,128)(2,1)S(1)}, bf16[384,1152]{1,0:T(8,128)(2,1)S(1)}, u32[]{:S(2)}, u32[]{:S(2)}) collective-permute-start(bf16[384,1152]{1,0:T(8,128)(2,1)S(1)} %bitcast.67), channel_id=1, source_target_pairs={{0,24},{24,0},{1,25},{25,1},{2,26},{26,2},{3,27},{27,3},{4,28},{28... | collective-permute-start | bytes 2654216 | tf_op jit(solution)/shard_map/ppermute | solution.py:37
  28.7 0.2 maximum_convert_fusion
  28.9 0.2 fusion.2
  29.1 1.6 %collective-permute-done = bf16[384,1152]{1,0:T(8,128)(2,1)S(1)} collective-permute-done((bf16[384,1152]{1,0:T(8,128)(2,1)S(1)}, bf16[384,1152]{1,0:T(8,128)(2,1)S(1)}, u32[]{:S(2)}, u32[]{:S(2)}) %collective-permute-start) | collective-permute-done | bytes 884768 | tf_op jit(solution)/shard_map/ppermute | solution.py:37
  30.8 0.4 fusion
  31.2 1.6 %divide_convert_fusion = bf16[576,768]{1,0:T(8,128)(2,1)S(1)} fusion(bf16[576,1152]{1,0:T(8,128)(2,1)S(1)} %fusion.2, f32[]{:T(128)} %bitcast.58, f32[]{:T(128)} %bitcast.9, f32[768]{0:T(1024)S(1)} %add_rsqrt_fusion.1, bf16[384,1152]{1,0:T(8,128)(2,1)S(1)} %collective-permute-done, bf16[384,1152]{1,0:T(8,128)(2,1)S(1)} %bitcast.69), kind=kOutput, calls=%fused_computation.11 | convolution fusion | flops 1027178496 | bytes 3984392 | tf_op jit(solution)/shard_map/dot_general | solution.py:92
  32.9 1.7 %convolution_convert_fusion.1 = bf16[288,1152]{1,0:T(8,128)(2,1)} fusion(bf16[576,768]{1,0:T(8,128)(2,1)S(1)} %divide_convert_fusion, f32[768]{0:T(1024)S(1)} %add_rsqrt_fusion.1, bf16[384,1152]{1,0:T(8,128)(2,1)S(1)} %collective-permute-done, bf16[384,1152]{1,0:T(8,128)(2,1)S(1)} %bitcast.70), kind=kOutput, calls=%fused_computation.8 | convolution fusion | flops 515248128 | bytes 2879488 | tf_op jit(solution)/shard_map/dot_general | solution.py:96
  34.6 5.2 %collective-permute-start.1 = (bf16[288,1152]{1,0:T(8,128)(2,1)}, bf16[288,1152]{1,0:T(8,128)(2,1)}, u32[]{:S(2)}, u32[]{:S(2)}) collective-permute-start(bf16[288,1152]{1,0:T(8,128)(2,1)} %convolution_convert_fusion.1), channel_id=1, source_target_pairs={{0,1},{1,0},{2,3},{3,2},{4,5},{5,4},{6,7},{7,6},{8,9},{9,8},{10,11... | collective-permute-start | bytes 1990664 | tf_op jit(solution)/shard_map/ppermute | solution.py:98
  39.9 0.1 fusion.27
  40.0 2.0 %convolution_convert_fusion = bf16[384,1152]{1,0:T(8,128)(2,1)S(1)} fusion(bf16[576,1152]{1,0:T(8,128)(2,1)S(1)} %fusion.2, bf16[576,768]{1,0:T(8,128)(2,1)} %copy-done.4), kind=kOutput, calls=%fused_computation.4 | convolution fusion | flops 510050304 | bytes 2654208 | tf_op jit(solution)/shard_map/ic,ie->ce/dot_general | solution.py:99
  42.1 1.9 %collective-permute-start.3 = (bf16[384,1152]{1,0:T(8,128)(2,1)S(1)}, bf16[384,1152]{1,0:T(8,128)(2,1)S(1)}, u32[]{:S(2)}, u32[]{:S(2)}) collective-permute-start(bf16[384,1152]{1,0:T(8,128)(2,1)S(1)} %convolution_convert_fusion), channel_id=1, source_target_pairs={{0,24},{24,0},{1,25},{25,1},{2,26},{26,2},{3,27},{27,3},{4,28},{28... | collective-permute-start | bytes 2654216 | tf_op jit(solution)/shard_map/ppermute | solution.py:37
  44.0 0.9 fusion.12
  44.9 3.9 %collective-permute-done.1 = bf16[288,1152]{1,0:T(8,128)(2,1)} collective-permute-done((bf16[288,1152]{1,0:T(8,128)(2,1)}, bf16[288,1152]{1,0:T(8,128)(2,1)}, u32[]{:S(2)}, u32[]{:S(2)}) %collective-permute-start.1) | collective-permute-done | bytes 663584 | tf_op jit(solution)/shard_map/ppermute | solution.py:98
  48.8 1.2 %convert_add_fusion.1 = f32[288,1152]{1,0:T(8,128)S(1)} fusion(f32[288,1152]{1,0:T(8,128)S(1)} %fusion.12, bf16[288,1152]{1,0:T(8,128)(2,1)} %collective-permute-done.1), kind=kLoop, calls=%fused_computation.13 | loop fusion | flops 663552 | bytes 3317760 | tf_op jit(solution)/shard_map/add | solution.py:105
  50.0 4.8 %collective-permute-start.2 = (bf16[6,24,1152]{2,1,0:T(8,128)(2,1)S(1)}, bf16[6,24,1152]{2,1,0:T(8,128)(2,1)S(1)}, u32[]{:S(2)}, u32[]{:S(2)}) collective-permute-start(bf16[6,24,1152]{2,1,0:T(8,128)(2,1)S(1)} %fusion.14), channel_id=1, source_target_pairs={{0,2},{1,3},{2,0},{3,1},{4,6},{5,7},{6,4},{7,5},{8,10},{9,11},{10,... | collective-permute-start | bytes 995336 | tf_op jit(solution)/shard_map/ppermute | solution.py:106
  54.8 0.0 collective-permute-done.3
  54.9 0.9 convert_add_fusion
  55.8 0.1 fusion.15
  55.9 4.4 %collective-permute-start.6 = (bf16[4,24,1152]{2,1,0:T(8,128)(2,1)S(1)}, bf16[4,24,1152]{2,1,0:T(8,128)(2,1)S(1)}, u32[]{:S(2)}, u32[]{:S(2)}) collective-permute-start(bf16[4,24,1152]{2,1,0:T(8,128)(2,1)S(1)} %get-tuple-element.14), channel_id=1, source_target_pairs={{0,144},{48,96},{96,48},{144,0},{192,336},{240,288},{288,240},{336... | collective-permute-start | bytes 663560 | tf_op jit(solution)/shard_map/ppermute | solution.py:68
  60.3 2.8 %collective-permute-start.5 = (bf16[4,24,1152]{2,1,0:T(8,128)(2,1)S(1)}, bf16[4,24,1152]{2,1,0:T(8,128)(2,1)S(1)}, u32[]{:S(2)}, u32[]{:S(2)}) collective-permute-start(bf16[4,24,1152]{2,1,0:T(8,128)(2,1)S(1)} %get-tuple-element.15), channel_id=1, source_target_pairs={{0,96},{48,144},{96,0},{144,48},{192,288},{240,336},{288,192},{336... | collective-permute-start | bytes 663560 | tf_op jit(solution)/shard_map/ppermute | solution.py:68
  63.1 2.6 %collective-permute-start.4 = (bf16[4,24,1152]{2,1,0:T(8,128)(2,1)S(1)}, bf16[4,24,1152]{2,1,0:T(8,128)(2,1)S(1)}, u32[]{:S(2)}, u32[]{:S(2)}) collective-permute-start(bf16[4,24,1152]{2,1,0:T(8,128)(2,1)S(1)} %get-tuple-element.13), channel_id=1, source_target_pairs={{0,48},{48,0},{96,144},{144,96},{192,240},{240,192},{288,336},{336... | collective-permute-start | bytes 663560 | tf_op jit(solution)/shard_map/ppermute | solution.py:68
  65.7 0.0 collective-permute-done.2
  65.7 0.8 fusion.3
  66.5 14.7 %all-to-all-start.1 = ((bf16[6,24,1152]{2,1,0:T(8,128)(2,1)}), bf16[6,24,1152]{2,1,0:T(8,128)(2,1)S(1)}, u32[]{:S(2)}, u32[]{:S(2)}) async-start(bf16[6,24,1152]{2,1,0:T(8,128)(2,1)} %fusion.3), calls=%async_computation.1 | async-start | bytes 663552 | tf_op jit(solution)/shard_map/all_to_all | solution.py:108
  81.3 0.0 collective-permute-done.6
  81.3 0.0 collective-permute-done.5
  81.3 0.0 collective-permute-done.4
  81.3 0.1 fusion.6
  81.5 6.5 %collective-permute-start.9 = (bf16[24,1152]{1,0:T(8,128)(2,1)S(1)}, bf16[24,1152]{1,0:T(8,128)(2,1)S(1)}, u32[]{:S(2)}, u32[]{:S(2)}) collective-permute-start(bf16[24,1152]{1,0:T(8,128)(2,1)S(1)} %get-tuple-element.19), channel_id=1, source_target_pairs={{0,576},{48,624},{96,672},{144,720},{192,384},{240,432},{288,480},... | collective-permute-start | bytes 165896 | tf_op jit(solution)/shard_map/ppermute | solution.py:68
  87.9 1.9 %collective-permute-start.8 = (bf16[24,1152]{1,0:T(8,128)(2,1)S(1)}, bf16[24,1152]{1,0:T(8,128)(2,1)S(1)}, u32[]{:S(2)}, u32[]{:S(2)}) collective-permute-start(bf16[24,1152]{1,0:T(8,128)(2,1)S(1)} %get-tuple-element.20), channel_id=1, source_target_pairs={{0,384},{48,432},{96,480},{144,528},{192,576},{240,624},{288,672},... | collective-permute-start | bytes 165896 | tf_op jit(solution)/shard_map/ppermute | solution.py:68
  89.9 2.5 %collective-permute-start.7 = (bf16[24,1152]{1,0:T(8,128)(2,1)S(1)}, bf16[24,1152]{1,0:T(8,128)(2,1)S(1)}, u32[]{:S(2)}, u32[]{:S(2)}) collective-permute-start(bf16[24,1152]{1,0:T(8,128)(2,1)S(1)} %get-tuple-element.18), channel_id=1, source_target_pairs={{0,192},{48,240},{96,288},{144,336},{192,0},{240,48},{288,96},{336... | collective-permute-start | bytes 165896 | tf_op jit(solution)/shard_map/ppermute | solution.py:68
  92.3 8.6 %all-to-all-done.1 = bf16[6,24,1152]{2,1,0:T(8,128)(2,1)S(1)} async-done(((bf16[6,24,1152]{2,1,0:T(8,128)(2,1)}), bf16[6,24,1152]{2,1,0:T(8,128)(2,1)S(1)}, u32[]{:S(2)}, u32[]{:S(2)}) %all-to-all-start.1) | async-done | bytes 331808 | tf_op jit(solution)/shard_map/all_to_all | solution.py:108
  101.0 0.0 collective-permute-done.9
  101.0 0.0 collective-permute-done.8
  101.0 0.0 collective-permute-done.7
  101.0 1.0 %fusion.28 = (f32[24]{0:T(128)S(1)}, f32[24]{0:T(128)S(1)}, f32[24,1152]{1,0:T(8,128)S(1)}) fusion(bf16[24,1152]{1,0:T(8,128)(2,1)S(1)} %copy-done.3, f32[24]{0:T(128)S(1)} %add_rsqrt_fusion.2, f32[]{:T(128)} %bitcast.9, f32[24,1152]{1,0:T(8,128)S(1)} %convert_reduce_fusion, f32[24]{0:T(128)S(1)} %add_rsqrt_fusion.3, bf16[576,1152]{1,0:T(8,128)(2,1)} %param.4, ...), kind=kLoop, calls=%fused_computation.48 | loop fusion | flops 608208 | bytes 608652 | tf_op jit(solution)/shard_map/reduce_sum | solution.py:20
  102.0 1.6 %fusion.30 = (f32[24,1152]{1,0:T(8,128)}, f32[24,1152]{1,0:T(8,128)}) fusion(f32[24,1152]{1,0:T(8,128)S(1)} %get-tuple-element.12, bf16[24,1152]{1,0:T(8,128)(2,1)S(1)} %copy-done.3, f32[24]{0:T(128)S(1)} %get-tuple-element.10, f32[24]{0:T(128)S(1)} %add_rsqrt_fusion.2, f32[24]{0:T(128)S(1)} %get-tuple-element.11, bf16[576,1152]{1,0:T(8,128)(2,1)} %param.4, ...), kind=kLoop, calls=%fused_computation.50 | loop fusion | flops 387072 | bytes 553352 | tf_op jit(solution)/shard_map/mul | solution.py:21
  (17 shorter events, 0.2 us)
Async XLA Ops:
  0.6 10.1 %copy-start = (bf16[576,1152]{1,0:T(8,128)(2,1)S(1)}, bf16[576,1152]{1,0:T(8,128)(2,1)}, u32[]{:S(2)}) copy-start(bf16[576,1152]{1,0:T(8,128)(2,1)} %param.4) | copy-start | bytes 3981316
  2.5 23.8 %all-to-all-start = ((bf16[16,24,1152]{2,1,0:T(8,128)(2,1)}), bf16[16,24,1152]{2,1,0:T(8,128)(2,1)S(1)}, u32[]{:S(2)}, u32[]{:S(2)}) async-start(bf16[16,24,1152]{2,1,0:T(8,128)(2,1)} %broadcast_in_dim.2), calls=%async_computation | async-start | bytes 1769472 | tf_op jit(solution)/shard_map/all_to_all | solution.py:60
  26.3 4.5 %collective-permute-start = (bf16[384,1152]{1,0:T(8,128)(2,1)S(1)}, bf16[384,1152]{1,0:T(8,128)(2,1)S(1)}, u32[]{:S(2)}, u32[]{:S(2)}) collective-permute-start(bf16[384,1152]{1,0:T(8,128)(2,1)S(1)} %bitcast.67), channel_id=1, source_target_pairs={{0,24},{24,0},{1,25},{25,1},{2,26},{26,2},{3,27},{27,3},{4,28},{28... | collective-permute-start | bytes 2654216 | tf_op jit(solution)/shard_map/ppermute | solution.py:37
  30.8 2.1 %copy-start.1 = (bf16[384,1152]{1,0:T(8,128)(2,1)}, bf16[384,1152]{1,0:T(8,128)(2,1)S(1)}, u32[]{:S(2)}) copy-start(bf16[384,1152]{1,0:T(8,128)(2,1)S(1)} %collective-permute-done) | copy-start | bytes 2654212
  32.8 1.7 %copy-start.4 = (bf16[576,768]{1,0:T(8,128)(2,1)}, bf16[576,768]{1,0:T(8,128)(2,1)S(1)}, u32[]{:S(2)}) copy-start(bf16[576,768]{1,0:T(8,128)(2,1)S(1)} %divide_convert_fusion) | copy-start | bytes 2654212
  34.6 14.2 %collective-permute-start.1 = (bf16[288,1152]{1,0:T(8,128)(2,1)}, bf16[288,1152]{1,0:T(8,128)(2,1)}, u32[]{:S(2)}, u32[]{:S(2)}) collective-permute-start(bf16[288,1152]{1,0:T(8,128)(2,1)} %convolution_convert_fusion.1), channel_id=1, source_target_pairs={{0,1},{1,0},{2,3},{3,2},{4,5},{5,4},{6,7},{7,6},{8,9},{9,8},{10,11... | collective-permute-start | bytes 1990664 | tf_op jit(solution)/shard_map/ppermute | solution.py:98
  39.9 4.1 %copy-start.2 = (bf16[384,1152]{1,0:T(8,128)(2,1)S(1)}, bf16[384,1152]{1,0:T(8,128)(2,1)}, u32[]{:S(2)}) copy-start(bf16[384,1152]{1,0:T(8,128)(2,1)} %copy-done.1) | copy-start | bytes 2654212
  39.9 4.1 %copy-start.5 = (bf16[576,768]{1,0:T(8,128)(2,1)S(1)}, bf16[576,768]{1,0:T(8,128)(2,1)}, u32[]{:S(2)}) copy-start(bf16[576,768]{1,0:T(8,128)(2,1)} %copy-done.4) | copy-start | bytes 2654212
  42.1 12.8 %collective-permute-start.3 = (bf16[384,1152]{1,0:T(8,128)(2,1)S(1)}, bf16[384,1152]{1,0:T(8,128)(2,1)S(1)}, u32[]{:S(2)}, u32[]{:S(2)}) collective-permute-start(bf16[384,1152]{1,0:T(8,128)(2,1)S(1)} %convolution_convert_fusion), channel_id=1, source_target_pairs={{0,24},{24,0},{1,25},{25,1},{2,26},{26,2},{3,27},{27,3},{4,28},{28... | collective-permute-start | bytes 2654216 | tf_op jit(solution)/shard_map/ppermute | solution.py:37
  50.0 15.7 %collective-permute-start.2 = (bf16[6,24,1152]{2,1,0:T(8,128)(2,1)S(1)}, bf16[6,24,1152]{2,1,0:T(8,128)(2,1)S(1)}, u32[]{:S(2)}, u32[]{:S(2)}) collective-permute-start(bf16[6,24,1152]{2,1,0:T(8,128)(2,1)S(1)} %fusion.14), channel_id=1, source_target_pairs={{0,2},{1,3},{2,0},{3,1},{4,6},{5,7},{6,4},{7,5},{8,10},{9,11},{10,... | collective-permute-start | bytes 995336 | tf_op jit(solution)/shard_map/ppermute | solution.py:106
  55.9 25.4 %collective-permute-start.6 = (bf16[4,24,1152]{2,1,0:T(8,128)(2,1)S(1)}, bf16[4,24,1152]{2,1,0:T(8,128)(2,1)S(1)}, u32[]{:S(2)}, u32[]{:S(2)}) collective-permute-start(bf16[4,24,1152]{2,1,0:T(8,128)(2,1)S(1)} %get-tuple-element.14), channel_id=1, source_target_pairs={{0,144},{48,96},{96,48},{144,0},{192,336},{240,288},{288,240},{336... | collective-permute-start | bytes 663560 | tf_op jit(solution)/shard_map/ppermute | solution.py:68
  60.3 21.0 %collective-permute-start.5 = (bf16[4,24,1152]{2,1,0:T(8,128)(2,1)S(1)}, bf16[4,24,1152]{2,1,0:T(8,128)(2,1)S(1)}, u32[]{:S(2)}, u32[]{:S(2)}) collective-permute-start(bf16[4,24,1152]{2,1,0:T(8,128)(2,1)S(1)} %get-tuple-element.15), channel_id=1, source_target_pairs={{0,96},{48,144},{96,0},{144,48},{192,288},{240,336},{288,192},{336... | collective-permute-start | bytes 663560 | tf_op jit(solution)/shard_map/ppermute | solution.py:68
  63.1 18.2 %collective-permute-start.4 = (bf16[4,24,1152]{2,1,0:T(8,128)(2,1)S(1)}, bf16[4,24,1152]{2,1,0:T(8,128)(2,1)S(1)}, u32[]{:S(2)}, u32[]{:S(2)}) collective-permute-start(bf16[4,24,1152]{2,1,0:T(8,128)(2,1)S(1)} %get-tuple-element.13), channel_id=1, source_target_pairs={{0,48},{48,0},{96,144},{144,96},{192,240},{240,192},{288,336},{336... | collective-permute-start | bytes 663560 | tf_op jit(solution)/shard_map/ppermute | solution.py:68
  66.5 34.5 %copy-start.3 = (bf16[24,1152]{1,0:T(8,128)(2,1)S(1)}, bf16[24,1152]{1,0:T(8,128)(2,1)}, u32[]{:S(2)}) copy-start(bf16[24,1152]{1,0:T(8,128)(2,1)} %param.5) | copy-start | bytes 165892
  66.5 34.4 %all-to-all-start.1 = ((bf16[6,24,1152]{2,1,0:T(8,128)(2,1)}), bf16[6,24,1152]{2,1,0:T(8,128)(2,1)S(1)}, u32[]{:S(2)}, u32[]{:S(2)}) async-start(bf16[6,24,1152]{2,1,0:T(8,128)(2,1)} %fusion.3), calls=%async_computation.1 | async-start | bytes 663552 | tf_op jit(solution)/shard_map/all_to_all | solution.py:108
  81.5 19.5 %collective-permute-start.9 = (bf16[24,1152]{1,0:T(8,128)(2,1)S(1)}, bf16[24,1152]{1,0:T(8,128)(2,1)S(1)}, u32[]{:S(2)}, u32[]{:S(2)}) collective-permute-start(bf16[24,1152]{1,0:T(8,128)(2,1)S(1)} %get-tuple-element.19), channel_id=1, source_target_pairs={{0,576},{48,624},{96,672},{144,720},{192,384},{240,432},{288,480},... | collective-permute-start | bytes 165896 | tf_op jit(solution)/shard_map/ppermute | solution.py:68
  87.9 13.0 %collective-permute-start.8 = (bf16[24,1152]{1,0:T(8,128)(2,1)S(1)}, bf16[24,1152]{1,0:T(8,128)(2,1)S(1)}, u32[]{:S(2)}, u32[]{:S(2)}) collective-permute-start(bf16[24,1152]{1,0:T(8,128)(2,1)S(1)} %get-tuple-element.20), channel_id=1, source_target_pairs={{0,384},{48,432},{96,480},{144,528},{192,576},{240,624},{288,672},... | collective-permute-start | bytes 165896 | tf_op jit(solution)/shard_map/ppermute | solution.py:68
  89.9 11.1 %collective-permute-start.7 = (bf16[24,1152]{1,0:T(8,128)(2,1)S(1)}, bf16[24,1152]{1,0:T(8,128)(2,1)S(1)}, u32[]{:S(2)}, u32[]{:S(2)}) collective-permute-start(bf16[24,1152]{1,0:T(8,128)(2,1)S(1)} %get-tuple-element.18), channel_id=1, source_target_pairs={{0,192},{48,240},{96,288},{144,336},{192,0},{240,48},{288,96},{336... | collective-permute-start | bytes 165896 | tf_op jit(solution)/shard_map/ppermute | solution.py:68

commit v3 on v2

--- a/solution.py
+++ b/solution.py
@@ -88,7 +88,7 @@
     other = flip(own, "c", 1)
     text_rows = jnp.concatenate([own, other], 0)
     xn = normalize(image_rows)[0].astype(BF)
-    yn = normalize(text_rows)[0].astype(BF)
+    yn = lax.optimization_barrier(normalize(text_rows)[0].astype(BF))
     logits = jnp.dot(xn, yn.T, preferred_element_type=F32) * scale + bias[0]
     w = jax.nn.sigmoid(logits).astype(BF)
     half = xn.shape[0] // 2

time: 105 us -> 104 us (level)
  other arithmetic: 7.04 us -> 5.7 us
  local copies, waits for them, and re-layouts: 2.45 us -> 3.68 us
    unnamed x14 -> x16, local copies, waits for them, and re-layouts: 0.13 us -> 1.36 us
    add x1, other arithmetic: 1.23 us -> 0.14 us  [local(): gx = (gx_keep + gx_got.astype(F32)).reshape(2, 6, ROWS, width)]
where the time goes in v3:
time: 104 us; the launch traced here: 103 us
  starting transfers between devices  57.2 us (55%)
  waiting for transfers between devices  26.9 us (26%)
  matrix products  6.88 us (7%)
  other arithmetic  5.7 us (5%)
  local copies, waits for them, and re-layouts  3.68 us (4%)
  between operations  2.44 us (2%)
    ppermute x6, starting transfers between devices, scatter_sum(): lax.ppermute(pick(total, 0, at ^ d).astype(BF), PLANE, [(member(*m), memb...  20.7 us
    all_to_all x1, starting transfers between devices, local(): gx = lax.all_to_all(gx, ('yh', 'z3'), 0, 0)  14.7 us
    all_to_all x1, waiting for transfers between devices, gather(): own = lax.all_to_all(copies, PLANE, 0, 0, axis_index_groups=groups)  13.3 us
    all_to_all x1, waiting for transfers between devices, local(): gx = lax.all_to_all(gx, ('yh', 'z3'), 0, 0)  8.07 us
    all_to_all x1, starting transfers between devices, gather(): own = lax.all_to_all(copies, PLANE, 0, 0, axis_index_groups=groups)  7.44 us
    ppermute x1, starting transfers between devices, local(): gx_got = lax.ppermute(gx_send, ('c', 'z3', 'z2', 'z1'), pair_perm(12, 1))  5.22 us
    ppermute x1, starting transfers between devices, local(): lax.ppermute(pick(gx, 0, 1 - z2).astype(BF), ('c', 'z3', 'z2', 'z1'), pai...  4.79 us
    ppermute x2, starting transfers between devices, flip(): return lax.ppermute(value, axis, [(i, i ^ distance) for i in range(size)])  4.35 us
  transfers between devices with their start and end apart: 12, of which 4 were waited for; matrix products, arithmetic and copies ran while one was open for 8% of the time, Pallas kernels for 0%

profile of v3, /device:TPU:64, one launch (start us, length us, event | category | flops | bytes accessed | tf_op | source)
XLA Modules:
  0.0 102.7 jit_solution(8776821868217687306)
XLA Ops:
  0.6 1.9 %broadcast_in_dim.2 = bf16[16,24,1152]{2,1,0:T(8,128)(2,1)} broadcast(bf16[24,1152]{1,0:T(8,128)(2,1)} %param.5), dimensions={1,2} | broadcast | bytes 940032 | tf_op jit(solution)/shard_map/broadcast_in_dim | solution.py:59
  2.5 7.4 %all-to-all-start = ((bf16[16,24,1152]{2,1,0:T(8,128)(2,1)}), bf16[16,24,1152]{2,1,0:T(8,128)(2,1)S(1)}, u32[]{:S(2)}, u32[]{:S(2)}) async-start(bf16[16,24,1152]{2,1,0:T(8,128)(2,1)} %broadcast_in_dim.2), calls=%async_computation | async-start | bytes 1769472 | tf_op jit(solution)/shard_map/all_to_all | solution.py:60
  10.7 0.2 constant_dynamic-slice_fusion.1
  10.9 0.1 copy.11
  10.9 0.1 copy.10
  11.0 0.3 multiply_reduce_fusion
  11.3 0.1 rsqrt.37
  12.1 0.9 fusion.31
  13.0 13.3 %all-to-all-done = bf16[16,24,1152]{2,1,0:T(8,128)(2,1)S(1)} async-done(((bf16[16,24,1152]{2,1,0:T(8,128)(2,1)}), bf16[16,24,1152]{2,1,0:T(8,128)(2,1)S(1)}, u32[]{:S(2)}, u32[]{:S(2)}) %all-to-all-start) | async-done | bytes 884768 | tf_op jit(solution)/shard_map/all_to_all | solution.py:60
  26.3 2.4 %collective-permute-start = (bf16[384,1152]{1,0:T(8,128)(2,1)S(1)}, bf16[384,1152]{1,0:T(8,128)(2,1)S(1)}, u32[]{:S(2)}, u32[]{:S(2)}) collective-permute-start(bf16[384,1152]{1,0:T(8,128)(2,1)S(1)} %bitcast.62), channel_id=1, source_target_pairs={{0,24},{24,0},{1,25},{25,1},{2,26},{26,2},{3,27},{27,3},{4,28},{28... | collective-permute-start | bytes 2654216 | tf_op jit(solution)/shard_map/ppermute | solution.py:37
  28.8 0.2 maximum_convert_fusion
  28.9 0.2 fusion.2
  29.2 1.6 %collective-permute-done = bf16[384,1152]{1,0:T(8,128)(2,1)S(1)} collective-permute-done((bf16[384,1152]{1,0:T(8,128)(2,1)S(1)}, bf16[384,1152]{1,0:T(8,128)(2,1)S(1)}, u32[]{:S(2)}, u32[]{:S(2)}) %collective-permute-start) | collective-permute-done | bytes 884768 | tf_op jit(solution)/shard_map/ppermute | solution.py:37
  30.8 0.4 fusion
  31.2 0.4 fusion.1
  31.6 1.5 %divide_convert_fusion = bf16[576,768]{1,0:T(8,128)(2,1)S(1)} fusion(bf16[576,1152]{1,0:T(8,128)(2,1)S(1)} %fusion.2, bf16[768,1152]{1,0:T(8,128)(2,1)S(1)} %fusion.1, f32[]{:T(128)} %bitcast.61, f32[]{:T(128)} %bitcast.9), kind=kOutput, calls=%fused_computation.11 | convolution fusion | flops 1021870080 | bytes 3981320 | tf_op jit(solution)/shard_map/dot_general | solution.py:92
  33.1 1.6 %convolution_convert_fusion.1 = bf16[288,1152]{1,0:T(8,128)(2,1)} fusion(bf16[768,1152]{1,0:T(8,128)(2,1)S(1)} %fusion.1, bf16[576,768]{1,0:T(8,128)(2,1)S(1)} %divide_convert_fusion), kind=kOutput, calls=%fused_computation.8 | convolution fusion | flops 509939712 | bytes 2875392 | tf_op jit(solution)/shard_map/dot_general | solution.py:96
  34.7 5.2 %collective-permute-start.1 = (bf16[288,1152]{1,0:T(8,128)(2,1)}, bf16[288,1152]{1,0:T(8,128)(2,1)S(1)}, u32[]{:S(2)}, u32[]{:S(2)}) collective-permute-start(bf16[288,1152]{1,0:T(8,128)(2,1)} %convolution_convert_fusion.1), channel_id=1, source_target_pairs={{0,1},{1,0},{2,3},{3,2},{4,5},{5,4},{6,7},{7,6},{8,9},{9,8},{10,11... | collective-permute-start | bytes 1990664 | tf_op jit(solution)/shard_map/ppermute | solution.py:98
  40.0 0.1 fusion.27
  40.2 2.1 %convolution_convert_fusion = bf16[384,1152]{1,0:T(8,128)(2,1)S(1)} fusion(bf16[576,1152]{1,0:T(8,128)(2,1)S(1)} %fusion.2, bf16[576,768]{1,0:T(8,128)(2,1)} %copy-done.5), kind=kOutput, calls=%fused_computation.4 | convolution fusion | flops 510050304 | bytes 2654208 | tf_op jit(solution)/shard_map/ic,ie->ce/dot_general | solution.py:99
  42.3 1.9 %collective-permute-start.3 = (bf16[384,1152]{1,0:T(8,128)(2,1)S(1)}, bf16[384,1152]{1,0:T(8,128)(2,1)S(1)}, u32[]{:S(2)}, u32[]{:S(2)}) collective-permute-start(bf16[384,1152]{1,0:T(8,128)(2,1)S(1)} %convolution_convert_fusion), channel_id=1, source_target_pairs={{0,24},{24,0},{1,25},{25,1},{2,26},{26,2},{3,27},{27,3},{4,28},{28... | collective-permute-start | bytes 2654216 | tf_op jit(solution)/shard_map/ppermute | solution.py:37
  44.2 0.7 fusion.12
  45.0 3.8 %collective-permute-done.1 = bf16[288,1152]{1,0:T(8,128)(2,1)S(1)} collective-permute-done((bf16[288,1152]{1,0:T(8,128)(2,1)}, bf16[288,1152]{1,0:T(8,128)(2,1)S(1)}, u32[]{:S(2)}, u32[]{:S(2)}) %collective-permute-start.1) | collective-permute-done | bytes 663584 | tf_op jit(solution)/shard_map/ppermute | solution.py:98
  48.8 0.1 convert_add_fusion.1
  49.0 4.8 %collective-permute-start.2 = (bf16[6,24,1152]{2,1,0:T(8,128)(2,1)S(1)}, bf16[6,24,1152]{2,1,0:T(8,128)(2,1)S(1)}, u32[]{:S(2)}, u32[]{:S(2)}) collective-permute-start(bf16[6,24,1152]{2,1,0:T(8,128)(2,1)S(1)} %fusion.14), channel_id=1, source_target_pairs={{0,2},{1,3},{2,0},{3,1},{4,6},{5,7},{6,4},{7,5},{8,10},{9,11},{10,... | collective-permute-start | bytes 995336 | tf_op jit(solution)/shard_map/ppermute | solution.py:106
  53.8 0.0 collective-permute-done.3
  53.8 0.9 convert_add_fusion
  54.8 1.2 %copy-done = f32[384,1152]{1,0:T(8,128)} copy-done((f32[384,1152]{1,0:T(8,128)}, f32[384,1152]{1,0:T(8,128)S(1)}, u32[]{:S(2)}) %copy-start) | copy-done | bytes 1769496
  56.0 0.1 fusion.15
  56.1 4.4 %collective-permute-start.6 = (bf16[4,24,1152]{2,1,0:T(8,128)(2,1)S(1)}, bf16[4,24,1152]{2,1,0:T(8,128)(2,1)S(1)}, u32[]{:S(2)}, u32[]{:S(2)}) collective-permute-start(bf16[4,24,1152]{2,1,0:T(8,128)(2,1)S(1)} %get-tuple-element.14), channel_id=1, source_target_pairs={{0,144},{48,96},{96,48},{144,0},{192,336},{240,288},{288,240},{336... | collective-permute-start | bytes 663560 | tf_op jit(solution)/shard_map/ppermute | solution.py:68
  60.5 2.8 %collective-permute-start.5 = (bf16[4,24,1152]{2,1,0:T(8,128)(2,1)S(1)}, bf16[4,24,1152]{2,1,0:T(8,128)(2,1)S(1)}, u32[]{:S(2)}, u32[]{:S(2)}) collective-permute-start(bf16[4,24,1152]{2,1,0:T(8,128)(2,1)S(1)} %get-tuple-element.15), channel_id=1, source_target_pairs={{0,96},{48,144},{96,0},{144,48},{192,288},{240,336},{288,192},{336... | collective-permute-start | bytes 663560 | tf_op jit(solution)/shard_map/ppermute | solution.py:68
  63.3 2.6 %collective-permute-start.4 = (bf16[4,24,1152]{2,1,0:T(8,128)(2,1)S(1)}, bf16[4,24,1152]{2,1,0:T(8,128)(2,1)S(1)}, u32[]{:S(2)}, u32[]{:S(2)}) collective-permute-start(bf16[4,24,1152]{2,1,0:T(8,128)(2,1)S(1)} %get-tuple-element.13), channel_id=1, source_target_pairs={{0,48},{48,0},{96,144},{144,96},{192,240},{240,192},{288,336},{336... | collective-permute-start | bytes 663560 | tf_op jit(solution)/shard_map/ppermute | solution.py:68
  65.9 0.0 collective-permute-done.2
  65.9 0.8 fusion.3
  66.7 14.7 %all-to-all-start.1 = ((bf16[6,24,1152]{2,1,0:T(8,128)(2,1)}), bf16[6,24,1152]{2,1,0:T(8,128)(2,1)S(1)}, u32[]{:S(2)}, u32[]{:S(2)}) async-start(bf16[6,24,1152]{2,1,0:T(8,128)(2,1)} %fusion.3), calls=%async_computation.1 | async-start | bytes 663552 | tf_op jit(solution)/shard_map/all_to_all | solution.py:108
  81.5 0.0 collective-permute-done.6
  81.5 0.0 collective-permute-done.5
  81.5 0.0 collective-permute-done.4
  81.5 1.1 %fusion.6 = f32[4,24,1152]{2,1,0:T(8,128)S(1)} fusion(bf16[4,24,1152]{2,1,0:T(8,128)(2,1)S(1)} %collective-permute-done.6, bf16[4,24,1152]{2,1,0:T(8,128)(2,1)S(1)} %collective-permute-done.5, bf16[4,24,1152]{2,1,0:T(8,128)(2,1)S(1)} %collective-permute-done.4, f32[4,4,24,1152]{3,2,1,0:T(8,128)} %bitcast.70, s32[]{:T(128)S(6)} %select_n.55), kind=kLoop, calls=%fused_computation.21 | loop fusion | flops 663552 | bytes 1548292 | tf_op jit(solution)/shard_map/add | solution.py:75
  82.7 6.5 %collective-permute-start.9 = (bf16[24,1152]{1,0:T(8,128)(2,1)S(1)}, bf16[24,1152]{1,0:T(8,128)(2,1)S(1)}, u32[]{:S(2)}, u32[]{:S(2)}) collective-permute-start(bf16[24,1152]{1,0:T(8,128)(2,1)S(1)} %get-tuple-element.19), channel_id=1, source_target_pairs={{0,576},{48,624},{96,672},{144,720},{192,384},{240,432},{288,480},... | collective-permute-start | bytes 165896 | tf_op jit(solution)/shard_map/ppermute | solution.py:68
  89.1 1.9 %collective-permute-start.8 = (bf16[24,1152]{1,0:T(8,128)(2,1)S(1)}, bf16[24,1152]{1,0:T(8,128)(2,1)S(1)}, u32[]{:S(2)}, u32[]{:S(2)}) collective-permute-start(bf16[24,1152]{1,0:T(8,128)(2,1)S(1)} %get-tuple-element.20), channel_id=1, source_target_pairs={{0,384},{48,432},{96,480},{144,528},{192,576},{240,624},{288,672},... | collective-permute-start | bytes 165896 | tf_op jit(solution)/shard_map/ppermute | solution.py:68
  91.1 2.5 %collective-permute-start.7 = (bf16[24,1152]{1,0:T(8,128)(2,1)S(1)}, bf16[24,1152]{1,0:T(8,128)(2,1)S(1)}, u32[]{:S(2)}, u32[]{:S(2)}) collective-permute-start(bf16[24,1152]{1,0:T(8,128)(2,1)S(1)} %get-tuple-element.18), channel_id=1, source_target_pairs={{0,192},{48,240},{96,288},{144,336},{192,0},{240,48},{288,96},{336... | collective-permute-start | bytes 165896 | tf_op jit(solution)/shard_map/ppermute | solution.py:68
  93.6 8.1 %all-to-all-done.1 = bf16[6,24,1152]{2,1,0:T(8,128)(2,1)S(1)} async-done(((bf16[6,24,1152]{2,1,0:T(8,128)(2,1)}), bf16[6,24,1152]{2,1,0:T(8,128)(2,1)S(1)}, u32[]{:S(2)}, u32[]{:S(2)}) %all-to-all-start.1) | async-done | bytes 331808 | tf_op jit(solution)/shard_map/all_to_all | solution.py:108
  101.7 0.0 collective-permute-done.9
  101.7 0.0 collective-permute-done.8
  101.7 0.0 collective-permute-done.7
  101.7 0.2 fusion.28
  101.9 0.8 fusion.30
  (20 shorter events, 0.2 us)
Async XLA Ops:
  0.6 10.1 %copy-start.3 = (bf16[576,1152]{1,0:T(8,128)(2,1)S(1)}, bf16[576,1152]{1,0:T(8,128)(2,1)}, u32[]{:S(2)}) copy-start(bf16[576,1152]{1,0:T(8,128)(2,1)} %param.4) | copy-start | bytes 3981316
  2.5 23.8 %all-to-all-start = ((bf16[16,24,1152]{2,1,0:T(8,128)(2,1)}), bf16[16,24,1152]{2,1,0:T(8,128)(2,1)S(1)}, u32[]{:S(2)}, u32[]{:S(2)}) async-start(bf16[16,24,1152]{2,1,0:T(8,128)(2,1)} %broadcast_in_dim.2), calls=%async_computation | async-start | bytes 1769472 | tf_op jit(solution)/shard_map/all_to_all | solution.py:60
  26.3 4.5 %collective-permute-start = (bf16[384,1152]{1,0:T(8,128)(2,1)S(1)}, bf16[384,1152]{1,0:T(8,128)(2,1)S(1)}, u32[]{:S(2)}, u32[]{:S(2)}) collective-permute-start(bf16[384,1152]{1,0:T(8,128)(2,1)S(1)} %bitcast.62), channel_id=1, source_target_pairs={{0,24},{24,0},{1,25},{25,1},{2,26},{26,2},{3,27},{27,3},{4,28},{28... | collective-permute-start | bytes 2654216 | tf_op jit(solution)/shard_map/ppermute | solution.py:37
  31.6 1.5 %copy-start.1 = (bf16[768,1152]{1,0:T(8,128)(2,1)}, bf16[768,1152]{1,0:T(8,128)(2,1)S(1)}, u32[]{:S(2)}) copy-start(bf16[768,1152]{1,0:T(8,128)(2,1)S(1)} %fusion.1) | copy-start | bytes 5308420
  33.1 1.6 %copy-start.5 = (bf16[576,768]{1,0:T(8,128)(2,1)}, bf16[576,768]{1,0:T(8,128)(2,1)S(1)}, u32[]{:S(2)}) copy-start(bf16[576,768]{1,0:T(8,128)(2,1)S(1)} %divide_convert_fusion) | copy-start | bytes 2654212
  34.7 14.1 %collective-permute-start.1 = (bf16[288,1152]{1,0:T(8,128)(2,1)}, bf16[288,1152]{1,0:T(8,128)(2,1)S(1)}, u32[]{:S(2)}, u32[]{:S(2)}) collective-permute-start(bf16[288,1152]{1,0:T(8,128)(2,1)} %convolution_convert_fusion.1), channel_id=1, source_target_pairs={{0,1},{1,0},{2,3},{3,2},{4,5},{5,4},{6,7},{7,6},{8,9},{9,8},{10,11... | collective-permute-start | bytes 1990664 | tf_op jit(solution)/shard_map/ppermute | solution.py:98
  40.0 4.2 %copy-start.2 = (bf16[768,1152]{1,0:T(8,128)(2,1)S(1)}, bf16[768,1152]{1,0:T(8,128)(2,1)}, u32[]{:S(2)}) copy-start(bf16[768,1152]{1,0:T(8,128)(2,1)} %copy-done.1) | copy-start | bytes 5308420
  40.0 4.2 %copy-start.6 = (bf16[576,768]{1,0:T(8,128)(2,1)S(1)}, bf16[576,768]{1,0:T(8,128)(2,1)}, u32[]{:S(2)}) copy-start(bf16[576,768]{1,0:T(8,128)(2,1)} %copy-done.5) | copy-start | bytes 2654212
  42.3 11.5 %collective-permute-start.3 = (bf16[384,1152]{1,0:T(8,128)(2,1)S(1)}, bf16[384,1152]{1,0:T(8,128)(2,1)S(1)}, u32[]{:S(2)}, u32[]{:S(2)}) collective-permute-start(bf16[384,1152]{1,0:T(8,128)(2,1)S(1)} %convolution_convert_fusion), channel_id=1, source_target_pairs={{0,24},{24,0},{1,25},{25,1},{2,26},{26,2},{3,27},{27,3},{4,28},{28... | collective-permute-start | bytes 2654216 | tf_op jit(solution)/shard_map/ppermute | solution.py:37
  49.0 16.9 %collective-permute-start.2 = (bf16[6,24,1152]{2,1,0:T(8,128)(2,1)S(1)}, bf16[6,24,1152]{2,1,0:T(8,128)(2,1)S(1)}, u32[]{:S(2)}, u32[]{:S(2)}) collective-permute-start(bf16[6,24,1152]{2,1,0:T(8,128)(2,1)S(1)} %fusion.14), channel_id=1, source_target_pairs={{0,2},{1,3},{2,0},{3,1},{4,6},{5,7},{6,4},{7,5},{8,10},{9,11},{10,... | collective-permute-start | bytes 995336 | tf_op jit(solution)/shard_map/ppermute | solution.py:106
  54.8 1.2 %copy-start = (f32[384,1152]{1,0:T(8,128)}, f32[384,1152]{1,0:T(8,128)S(1)}, u32[]{:S(2)}) copy-start(f32[384,1152]{1,0:T(8,128)S(1)} %convert_add_fusion) | copy-start | bytes 5308420
  56.1 25.4 %collective-permute-start.6 = (bf16[4,24,1152]{2,1,0:T(8,128)(2,1)S(1)}, bf16[4,24,1152]{2,1,0:T(8,128)(2,1)S(1)}, u32[]{:S(2)}, u32[]{:S(2)}) collective-permute-start(bf16[4,24,1152]{2,1,0:T(8,128)(2,1)S(1)} %get-tuple-element.14), channel_id=1, source_target_pairs={{0,144},{48,96},{96,48},{144,0},{192,336},{240,288},{288,240},{336... | collective-permute-start | bytes 663560 | tf_op jit(solution)/shard_map/ppermute | solution.py:68
  60.5 21.0 %collective-permute-start.5 = (bf16[4,24,1152]{2,1,0:T(8,128)(2,1)S(1)}, bf16[4,24,1152]{2,1,0:T(8,128)(2,1)S(1)}, u32[]{:S(2)}, u32[]{:S(2)}) collective-permute-start(bf16[4,24,1152]{2,1,0:T(8,128)(2,1)S(1)} %get-tuple-element.15), channel_id=1, source_target_pairs={{0,96},{48,144},{96,0},{144,48},{192,288},{240,336},{288,192},{336... | collective-permute-start | bytes 663560 | tf_op jit(solution)/shard_map/ppermute | solution.py:68
  63.3 18.2 %collective-permute-start.4 = (bf16[4,24,1152]{2,1,0:T(8,128)(2,1)S(1)}, bf16[4,24,1152]{2,1,0:T(8,128)(2,1)S(1)}, u32[]{:S(2)}, u32[]{:S(2)}) collective-permute-start(bf16[4,24,1152]{2,1,0:T(8,128)(2,1)S(1)} %get-tuple-element.13), channel_id=1, source_target_pairs={{0,48},{48,0},{96,144},{144,96},{192,240},{240,192},{288,336},{336... | collective-permute-start | bytes 663560 | tf_op jit(solution)/shard_map/ppermute | solution.py:68
  66.7 35.0 %copy-start.4 = (bf16[24,1152]{1,0:T(8,128)(2,1)S(1)}, bf16[24,1152]{1,0:T(8,128)(2,1)}, u32[]{:S(2)}) copy-start(bf16[24,1152]{1,0:T(8,128)(2,1)} %param.5) | copy-start | bytes 165892
  66.7 34.9 %all-to-all-start.1 = ((bf16[6,24,1152]{2,1,0:T(8,128)(2,1)}), bf16[6,24,1152]{2,1,0:T(8,128)(2,1)S(1)}, u32[]{:S(2)}, u32[]{:S(2)}) async-start(bf16[6,24,1152]{2,1,0:T(8,128)(2,1)} %fusion.3), calls=%async_computation.1 | async-start | bytes 663552 | tf_op jit(solution)/shard_map/all_to_all | solution.py:108
  82.7 19.0 %collective-permute-start.9 = (bf16[24,1152]{1,0:T(8,128)(2,1)S(1)}, bf16[24,1152]{1,0:T(8,128)(2,1)S(1)}, u32[]{:S(2)}, u32[]{:S(2)}) collective-permute-start(bf16[24,1152]{1,0:T(8,128)(2,1)S(1)} %get-tuple-element.19), channel_id=1, source_target_pairs={{0,576},{48,624},{96,672},{144,720},{192,384},{240,432},{288,480},... | collective-permute-start | bytes 165896 | tf_op jit(solution)/shard_map/ppermute | solution.py:68
  89.1 12.5 %collective-permute-start.8 = (bf16[24,1152]{1,0:T(8,128)(2,1)S(1)}, bf16[24,1152]{1,0:T(8,128)(2,1)S(1)}, u32[]{:S(2)}, u32[]{:S(2)}) collective-permute-start(bf16[24,1152]{1,0:T(8,128)(2,1)S(1)} %get-tuple-element.20), channel_id=1, source_target_pairs={{0,384},{48,432},{96,480},{144,528},{192,576},{240,624},{288,672},... | collective-permute-start | bytes 165896 | tf_op jit(solution)/shard_map/ppermute | solution.py:68
  91.1 10.6 %collective-permute-start.7 = (bf16[24,1152]{1,0:T(8,128)(2,1)S(1)}, bf16[24,1152]{1,0:T(8,128)(2,1)S(1)}, u32[]{:S(2)}, u32[]{:S(2)}) collective-permute-start(bf16[24,1152]{1,0:T(8,128)(2,1)S(1)} %get-tuple-element.18), channel_id=1, source_target_pairs={{0,192},{48,240},{96,288},{144,336},{192,0},{240,48},{288,96},{336... | collective-permute-start | bytes 165896 | tf_op jit(solution)/shard_map/ppermute | solution.py:68

commit v4 on v3

--- a/solution.py
+++ b/solution.py
@@ -72,7 +72,7 @@
             )
             for d in (1, 2, 3)
         ]
-        total = pick(total, 0, at) + got[0].astype(F32) + got[1].astype(F32) + got[2].astype(F32)
+        total = pick(total, 0, at).astype(F32) + got[0].astype(F32) + got[1].astype(F32) + got[2].astype(F32)
     return total
 
 
@@ -106,10 +106,10 @@
     gx_got = lax.ppermute(pick(gx, 0, 1 - z2).astype(BF), ("c", "z3", "z2", "z1"), pair_perm(12, 2))
     gx = (pick(gx, 0, z2) + gx_got.astype(F32)).astype(BF)
     gx = lax.all_to_all(gx, ("yh", "z3"), 0, 0)
-    gy = (gy_own + gy_got.astype(F32)).reshape(4, 4, ROWS, width)
+    gy = (gy_own + gy_got.astype(F32)).astype(BF).reshape(4, 4, ROWS, width)
     gy = scatter_sum(gy)
     gx = jnp.sum(gx.astype(F32), 0)
-    own_images = lax.dynamic_slice_in_dim(images, group * ROWS, ROWS, 0)
+    own_images = lax.optimization_barrier(lax.dynamic_slice_in_dim(images, group * ROWS, ROWS, 0))
     unit_x, inv_x = normalize(own_images)
     unit_y, inv_y = normalize(texts)
     gx = (gx - unit_y.astype(BF).astype(F32)) * scale

time: 104 us -> 105 us (level)
  the two profiles are of different devices: /device:TPU:64 before, /device:TPU:68 now
where the time goes in v4:
time: 105 us; the launch traced here: 104 us
  starting transfers between devices  57.4 us (55%)
  waiting for transfers between devices  26.7 us (25%)
  other arithmetic  9.44 us (9%)
  matrix products  4.85 us (5%)
  local copies, waits for them, and re-layouts  3.72 us (4%)
  between operations  2.4 us (2%)
    ppermute x6, starting transfers between devices, scatter_sum(): lax.ppermute(pick(total, 0, at ^ d).astype(BF), PLANE, [(member(*m), memb...  20.1 us
    all_to_all x1, starting transfers between devices, local(): gx = lax.all_to_all(gx, ('yh', 'z3'), 0, 0)  15.3 us
    all_to_all x1, waiting for transfers between devices, gather(): own = lax.all_to_all(copies, PLANE, 0, 0, axis_index_groups=groups)  12.4 us
    all_to_all x1, waiting for transfers between devices, local(): gx = lax.all_to_all(gx, ('yh', 'z3'), 0, 0)  9.31 us
    all_to_all x1, starting transfers between devices, gather(): own = lax.all_to_all(copies, PLANE, 0, 0, axis_index_groups=groups)  7.86 us
    ppermute x1, starting transfers between devices, local(): lax.ppermute(pick(gx, 0, 1 - z2).astype(BF), ('c', 'z3', 'z2', 'z1'), pai...  5.58 us
    ppermute x1, waiting for transfers between devices, local(): gx_got = lax.ppermute(gx_send, ('c', 'z3', 'z2', 'z1'), pair_perm(12, 1))  4.89 us
    ppermute x1, starting transfers between devices, local(): gx_got = lax.ppermute(gx_send, ('c', 'z3', 'z2', 'z1'), pair_perm(12, 1))  4.43 us
  transfers between devices with their start and end apart: 12, of which 3 were waited for; matrix products, arithmetic and copies ran while one was open for 9% of the time, Pallas kernels for 0%

profile of v4, /device:TPU:68, one launch (start us, length us, event | category | flops | bytes accessed | tf_op | source)
XLA Modules:
  0.0 104.4 jit_solution(11821348845799783454)
XLA Ops:
  0.6 1.9 %broadcast_in_dim.2 = bf16[16,24,1152]{2,1,0:T(8,128)(2,1)} broadcast(bf16[24,1152]{1,0:T(8,128)(2,1)} %param.5), dimensions={1,2} | broadcast | bytes 940032 | tf_op jit(solution)/shard_map/broadcast_in_dim | solution.py:59
  2.5 7.9 %all-to-all-start = ((bf16[16,24,1152]{2,1,0:T(8,128)(2,1)}), bf16[16,24,1152]{2,1,0:T(8,128)(2,1)S(1)}, u32[]{:S(2)}, u32[]{:S(2)}) async-start(bf16[16,24,1152]{2,1,0:T(8,128)(2,1)} %broadcast_in_dim.2), calls=%async_computation | async-start | bytes 1769472 | tf_op jit(solution)/shard_map/all_to_all | solution.py:60
  10.4 0.2 constant_dynamic-slice_fusion.1
  10.6 0.1 copy.11
  10.6 0.1 copy.10
  10.7 0.3 multiply_reduce_fusion
  11.1 0.4 copy-done
  11.5 0.2 copy-done.1
  11.7 0.6 constant_dynamic-slice_fusion.2
  12.4 1.5 %maximum_convert_fusion = f32[24,24,1152]{2,1,0:T(8,128)S(1)} fusion(bf16[12,24,1152]{2,1,0:T(8,128)(2,1)} %bitcast.63, bf16[12,24,1152]{2,1,0:T(8,128)(2,1)} %bitcast.65), kind=kLoop, calls=%fused_computation.12 | loop fusion | flops 1327104 | bytes 3981312 | tf_op jit(solution)/shard_map/convert_element_type | solution.py:14
  13.8 12.4 %all-to-all-done = bf16[16,24,1152]{2,1,0:T(8,128)(2,1)S(1)} async-done(((bf16[16,24,1152]{2,1,0:T(8,128)(2,1)}), bf16[16,24,1152]{2,1,0:T(8,128)(2,1)S(1)}, u32[]{:S(2)}, u32[]{:S(2)}) %all-to-all-start) | async-done | bytes 884768 | tf_op jit(solution)/shard_map/all_to_all | solution.py:60
  26.3 2.2 %collective-permute-start = (bf16[384,1152]{1,0:T(8,128)(2,1)S(1)}, bf16[384,1152]{1,0:T(8,128)(2,1)}, u32[]{:S(2)}, u32[]{:S(2)}) collective-permute-start(bf16[384,1152]{1,0:T(8,128)(2,1)S(1)} %bitcast.59), channel_id=1, source_target_pairs={{0,24},{24,0},{1,25},{25,1},{2,26},{26,2},{3,27},{27,3},{4,28},{28... | collective-permute-start | bytes 2654216 | tf_op jit(solution)/shard_map/ppermute | solution.py:37
  28.5 1.4 %fusion.28 = f32[24]{0:T(128)} fusion(bf16[24,1152]{1,0:T(8,128)(2,1)} %param.5), kind=kLoop, calls=%fused_computation.48 | loop fusion | flops 82920 | bytes 55392 | tf_op jit(solution)/shard_map/reduce_sum | solution.py:15
  30.7 0.1 rsqrt.37
  31.4 0.7 add_rsqrt_fusion.2
  32.1 0.2 fusion.2
  32.3 0.0 collective-permute-done
  32.3 1.6 %fusion = f32[768]{0:T(1024)S(1)} fusion(bf16[384,1152]{1,0:T(8,128)(2,1)} %collective-permute-done, bf16[384,1152]{1,0:T(8,128)(2,1)S(1)} %bitcast.60), kind=kLoop, calls=%fused_computation.2 | loop fusion | flops 5307648 | bytes 1772544 | tf_op jit(solution)/shard_map/reduce_sum | solution.py:15
  33.9 1.5 %fusion.1 = bf16[768,1152]{1,0:T(8,128)(2,1)S(1)} fusion(f32[768]{0:T(1024)S(1)} %add_rsqrt_fusion.1, bf16[384,1152]{1,0:T(8,128)(2,1)} %collective-permute-done, bf16[384,1152]{1,0:T(8,128)(2,1)S(1)} %bitcast.61), kind=kLoop, calls=%fused_computation.3 | loop fusion | flops 5308416 | bytes 3542016 | tf_op jit(solution)/shard_map/convert_element_type | solution.py:91
  35.4 1.5 %divide_convert_fusion = bf16[576,768]{1,0:T(8,128)(2,1)S(1)} fusion(bf16[576,1152]{1,0:T(8,128)(2,1)S(1)} %fusion.2, bf16[768,1152]{1,0:T(8,128)(2,1)S(1)} %fusion.1, f32[]{:T(128)} %bitcast.58, f32[]{:T(128)} %bitcast.9), kind=kOutput, calls=%fused_computation.11 | convolution fusion | flops 1021870080 | bytes 3981320 | tf_op jit(solution)/shard_map/dot_general | solution.py:92
  37.0 0.0 copy-start.3
  37.0 0.7 convolution_convert_fusion.1
  37.7 4.4 %collective-permute-start.1 = (bf16[288,1152]{1,0:T(8,128)(2,1)S(1)}, bf16[288,1152]{1,0:T(8,128)(2,1)S(1)}, u32[]{:S(2)}, u32[]{:S(2)}) collective-permute-start(bf16[288,1152]{1,0:T(8,128)(2,1)S(1)} %convolution_convert_fusion.1), channel_id=1, source_target_pairs={{0,1},{1,0},{2,3},{3,2},{4,5},{5,4},{6,7},{7,6},{8,9},{9,8},{10,11... | collective-permute-start | bytes 1990664 | tf_op jit(solution)/shard_map/ppermute | solution.py:98
  42.2 0.1 fusion.24
  42.3 0.9 convolution_convert_fusion
  43.2 1.9 %collective-permute-start.3 = (bf16[384,1152]{1,0:T(8,128)(2,1)S(1)}, bf16[384,1152]{1,0:T(8,128)(2,1)S(1)}, u32[]{:S(2)}, u32[]{:S(2)}) collective-permute-start(bf16[384,1152]{1,0:T(8,128)(2,1)S(1)} %convolution_convert_fusion), channel_id=1, source_target_pairs={{0,24},{24,0},{1,25},{25,1},{2,26},{26,2},{3,27},{27,3},{4,28},{28... | collective-permute-start | bytes 2654216 | tf_op jit(solution)/shard_map/ppermute | solution.py:37
  45.2 0.7 fusion.12
  45.9 4.9 %collective-permute-done.1 = bf16[288,1152]{1,0:T(8,128)(2,1)S(1)} collective-permute-done((bf16[288,1152]{1,0:T(8,128)(2,1)S(1)}, bf16[288,1152]{1,0:T(8,128)(2,1)S(1)}, u32[]{:S(2)}, u32[]{:S(2)}) %collective-permute-start.1) | collective-permute-done | bytes 663584 | tf_op jit(solution)/shard_map/ppermute | solution.py:98
  50.8 0.1 convert_add_fusion
  51.0 5.6 %collective-permute-start.2 = (bf16[6,24,1152]{2,1,0:T(8,128)(2,1)S(1)}, bf16[6,24,1152]{2,1,0:T(8,128)(2,1)S(1)}, u32[]{:S(2)}, u32[]{:S(2)}) collective-permute-start(bf16[6,24,1152]{2,1,0:T(8,128)(2,1)S(1)} %fusion.14), channel_id=1, source_target_pairs={{0,2},{1,3},{2,0},{3,1},{4,6},{5,7},{6,4},{7,5},{8,10},{9,11},{10,... | collective-permute-start | bytes 995336 | tf_op jit(solution)/shard_map/ppermute | solution.py:106
  56.6 0.9 add_convert_fusion
  57.5 0.1 dynamic-slice_bitcast_fusion.2
  57.6 2.5 %collective-permute-start.6 = (bf16[4,24,1152]{2,1,0:T(8,128)(2,1)S(1)}, bf16[4,24,1152]{2,1,0:T(8,128)(2,1)S(1)}, u32[]{:S(2)}, u32[]{:S(2)}) collective-permute-start(bf16[4,24,1152]{2,1,0:T(8,128)(2,1)S(1)} %get-tuple-element.16), channel_id=1, source_target_pairs={{0,144},{48,96},{96,48},{144,0},{192,336},{240,288},{288,240},{336... | collective-permute-start | bytes 663560 | tf_op jit(solution)/shard_map/ppermute | solution.py:68
  60.1 4.6 %collective-permute-start.5 = (bf16[4,24,1152]{2,1,0:T(8,128)(2,1)S(1)}, bf16[4,24,1152]{2,1,0:T(8,128)(2,1)S(1)}, u32[]{:S(2)}, u32[]{:S(2)}) collective-permute-start(bf16[4,24,1152]{2,1,0:T(8,128)(2,1)S(1)} %get-tuple-element.17), channel_id=1, source_target_pairs={{0,96},{48,144},{96,0},{144,48},{192,288},{240,336},{288,192},{336... | collective-permute-start | bytes 663560 | tf_op jit(solution)/shard_map/ppermute | solution.py:68
  64.7 0.0 copy-start.4
  64.7 2.9 %collective-permute-start.4 = (bf16[4,24,1152]{2,1,0:T(8,128)(2,1)S(1)}, bf16[4,24,1152]{2,1,0:T(8,128)(2,1)S(1)}, u32[]{:S(2)}, u32[]{:S(2)}) collective-permute-start(bf16[4,24,1152]{2,1,0:T(8,128)(2,1)S(1)} %get-tuple-element.15), channel_id=1, source_target_pairs={{0,48},{48,0},{96,144},{144,96},{192,240},{240,192},{288,336},{336... | collective-permute-start | bytes 663560 | tf_op jit(solution)/shard_map/ppermute | solution.py:68
  67.6 0.8 fusion.3
  68.4 15.3 %all-to-all-start.1 = ((bf16[6,24,1152]{2,1,0:T(8,128)(2,1)}), bf16[6,24,1152]{2,1,0:T(8,128)(2,1)S(1)}, u32[]{:S(2)}, u32[]{:S(2)}) async-start(bf16[6,24,1152]{2,1,0:T(8,128)(2,1)} %fusion.3), calls=%async_computation.1 | async-start | bytes 663552 | tf_op jit(solution)/shard_map/all_to_all | solution.py:108
  83.7 0.0 collective-permute-done.5
  83.7 0.1 fusion.6
  83.9 3.8 %collective-permute-start.9 = (bf16[24,1152]{1,0:T(8,128)(2,1)S(1)}, bf16[24,1152]{1,0:T(8,128)(2,1)S(1)}, u32[]{:S(2)}, u32[]{:S(2)}) collective-permute-start(bf16[24,1152]{1,0:T(8,128)(2,1)S(1)} %get-tuple-element.19), channel_id=1, source_target_pairs={{0,576},{48,624},{96,672},{144,720},{192,384},{240,432},{288,480},... | collective-permute-start | bytes 165896 | tf_op jit(solution)/shard_map/ppermute | solution.py:68
  87.7 2.3 %collective-permute-start.8 = (bf16[24,1152]{1,0:T(8,128)(2,1)S(1)}, bf16[24,1152]{1,0:T(8,128)(2,1)S(1)}, u32[]{:S(2)}, u32[]{:S(2)}) collective-permute-start(bf16[24,1152]{1,0:T(8,128)(2,1)S(1)} %get-tuple-element.20), channel_id=1, source_target_pairs={{0,384},{48,432},{96,480},{144,528},{192,576},{240,624},{288,672},... | collective-permute-start | bytes 165896 | tf_op jit(solution)/shard_map/ppermute | solution.py:68
  90.1 4.0 %collective-permute-start.7 = (bf16[24,1152]{1,0:T(8,128)(2,1)S(1)}, bf16[24,1152]{1,0:T(8,128)(2,1)S(1)}, u32[]{:S(2)}, u32[]{:S(2)}) collective-permute-start(bf16[24,1152]{1,0:T(8,128)(2,1)S(1)} %get-tuple-element.18), channel_id=1, source_target_pairs={{0,192},{48,240},{96,288},{144,336},{192,0},{240,48},{288,96},{336... | collective-permute-start | bytes 165896 | tf_op jit(solution)/shard_map/ppermute | solution.py:68
  94.0 9.3 %all-to-all-done.1 = bf16[6,24,1152]{2,1,0:T(8,128)(2,1)S(1)} async-done(((bf16[6,24,1152]{2,1,0:T(8,128)(2,1)}), bf16[6,24,1152]{2,1,0:T(8,128)(2,1)S(1)}, u32[]{:S(2)}, u32[]{:S(2)}) %all-to-all-start.1) | async-done | bytes 331808 | tf_op jit(solution)/shard_map/all_to_all | solution.py:108
  103.4 0.0 collective-permute-done.9
  103.4 0.0 collective-permute-done.8
  103.4 0.2 fusion.25
  103.6 0.8 fusion.27
  (17 shorter events, 0.2 us)
Async XLA Ops:
  0.6 9.8 %copy-start.2 = (bf16[576,1152]{1,0:T(8,128)(2,1)S(1)}, bf16[576,1152]{1,0:T(8,128)(2,1)}, u32[]{:S(2)}) copy-start(bf16[576,1152]{1,0:T(8,128)(2,1)} %param.4) | copy-start | bytes 3981316
  2.5 23.8 %all-to-all-start = ((bf16[16,24,1152]{2,1,0:T(8,128)(2,1)}), bf16[16,24,1152]{2,1,0:T(8,128)(2,1)S(1)}, u32[]{:S(2)}, u32[]{:S(2)}) async-start(bf16[16,24,1152]{2,1,0:T(8,128)(2,1)} %broadcast_in_dim.2), calls=%async_computation | async-start | bytes 1769472 | tf_op jit(solution)/shard_map/all_to_all | solution.py:60
  10.6 0.9 copy-start
  10.7 1.0 copy-start.1
  26.3 6.0 %collective-permute-start = (bf16[384,1152]{1,0:T(8,128)(2,1)S(1)}, bf16[384,1152]{1,0:T(8,128)(2,1)}, u32[]{:S(2)}, u32[]{:S(2)}) collective-permute-start(bf16[384,1152]{1,0:T(8,128)(2,1)S(1)} %bitcast.59), channel_id=1, source_target_pairs={{0,24},{24,0},{1,25},{25,1},{2,26},{26,2},{3,27},{27,3},{4,28},{28... | collective-permute-start | bytes 2654216 | tf_op jit(solution)/shard_map/ppermute | solution.py:37
  37.0 5.2 %copy-start.3 = (bf16[24,1152]{1,0:T(8,128)(2,1)S(1)}, bf16[24,1152]{1,0:T(8,128)(2,1)}, u32[]{:S(2)}) copy-start(bf16[24,1152]{1,0:T(8,128)(2,1)} %constant_dynamic-slice_fusion.2) | copy-start | bytes 165892
  37.7 13.1 %collective-permute-start.1 = (bf16[288,1152]{1,0:T(8,128)(2,1)S(1)}, bf16[288,1152]{1,0:T(8,128)(2,1)S(1)}, u32[]{:S(2)}, u32[]{:S(2)}) collective-permute-start(bf16[288,1152]{1,0:T(8,128)(2,1)S(1)} %convolution_convert_fusion.1), channel_id=1, source_target_pairs={{0,1},{1,0},{2,3},{3,2},{4,5},{5,4},{6,7},{7,6},{8,9},{9,8},{10,11... | collective-permute-start | bytes 1990664 | tf_op jit(solution)/shard_map/ppermute | solution.py:98
  43.2 13.3 %collective-permute-start.3 = (bf16[384,1152]{1,0:T(8,128)(2,1)S(1)}, bf16[384,1152]{1,0:T(8,128)(2,1)S(1)}, u32[]{:S(2)}, u32[]{:S(2)}) collective-permute-start(bf16[384,1152]{1,0:T(8,128)(2,1)S(1)} %convolution_convert_fusion), channel_id=1, source_target_pairs={{0,24},{24,0},{1,25},{25,1},{2,26},{26,2},{3,27},{27,3},{4,28},{28... | collective-permute-start | bytes 2654216 | tf_op jit(solution)/shard_map/ppermute | solution.py:37
  51.0 16.6 %collective-permute-start.2 = (bf16[6,24,1152]{2,1,0:T(8,128)(2,1)S(1)}, bf16[6,24,1152]{2,1,0:T(8,128)(2,1)S(1)}, u32[]{:S(2)}, u32[]{:S(2)}) collective-permute-start(bf16[6,24,1152]{2,1,0:T(8,128)(2,1)S(1)} %fusion.14), channel_id=1, source_target_pairs={{0,2},{1,3},{2,0},{3,1},{4,6},{5,7},{6,4},{7,5},{8,10},{9,11},{10,... | collective-permute-start | bytes 995336 | tf_op jit(solution)/shard_map/ppermute | solution.py:106
  57.6 26.1 %collective-permute-start.6 = (bf16[4,24,1152]{2,1,0:T(8,128)(2,1)S(1)}, bf16[4,24,1152]{2,1,0:T(8,128)(2,1)S(1)}, u32[]{:S(2)}, u32[]{:S(2)}) collective-permute-start(bf16[4,24,1152]{2,1,0:T(8,128)(2,1)S(1)} %get-tuple-element.16), channel_id=1, source_target_pairs={{0,144},{48,96},{96,48},{144,0},{192,336},{240,288},{288,240},{336... | collective-permute-start | bytes 663560 | tf_op jit(solution)/shard_map/ppermute | solution.py:68
  60.1 23.6 %collective-permute-start.5 = (bf16[4,24,1152]{2,1,0:T(8,128)(2,1)S(1)}, bf16[4,24,1152]{2,1,0:T(8,128)(2,1)S(1)}, u32[]{:S(2)}, u32[]{:S(2)}) collective-permute-start(bf16[4,24,1152]{2,1,0:T(8,128)(2,1)S(1)} %get-tuple-element.17), channel_id=1, source_target_pairs={{0,96},{48,144},{96,0},{144,48},{192,288},{240,336},{288,192},{336... | collective-permute-start | bytes 663560 | tf_op jit(solution)/shard_map/ppermute | solution.py:68
  64.7 38.8 %copy-start.4 = (bf16[24,1152]{1,0:T(8,128)(2,1)S(1)}, bf16[24,1152]{1,0:T(8,128)(2,1)}, u32[]{:S(2)}) copy-start(bf16[24,1152]{1,0:T(8,128)(2,1)} %param.5) | copy-start | bytes 165892
  64.7 19.0 %collective-permute-start.4 = (bf16[4,24,1152]{2,1,0:T(8,128)(2,1)S(1)}, bf16[4,24,1152]{2,1,0:T(8,128)(2,1)S(1)}, u32[]{:S(2)}, u32[]{:S(2)}) collective-permute-start(bf16[4,24,1152]{2,1,0:T(8,128)(2,1)S(1)} %get-tuple-element.15), channel_id=1, source_target_pairs={{0,48},{48,0},{96,144},{144,96},{192,240},{240,192},{288,336},{336... | collective-permute-start | bytes 663560 | tf_op jit(solution)/shard_map/ppermute | solution.py:68
  68.4 35.0 %all-to-all-start.1 = ((bf16[6,24,1152]{2,1,0:T(8,128)(2,1)}), bf16[6,24,1152]{2,1,0:T(8,128)(2,1)S(1)}, u32[]{:S(2)}, u32[]{:S(2)}) async-start(bf16[6,24,1152]{2,1,0:T(8,128)(2,1)} %fusion.3), calls=%async_computation.1 | async-start | bytes 663552 | tf_op jit(solution)/shard_map/all_to_all | solution.py:108
  83.9 19.5 %collective-permute-start.9 = (bf16[24,1152]{1,0:T(8,128)(2,1)S(1)}, bf16[24,1152]{1,0:T(8,128)(2,1)S(1)}, u32[]{:S(2)}, u32[]{:S(2)}) collective-permute-start(bf16[24,1152]{1,0:T(8,128)(2,1)S(1)} %get-tuple-element.19), channel_id=1, source_target_pairs={{0,576},{48,624},{96,672},{144,720},{192,384},{240,432},{288,480},... | collective-permute-start | bytes 165896 | tf_op jit(solution)/shard_map/ppermute | solution.py:68
  87.7 15.7 %collective-permute-start.8 = (bf16[24,1152]{1,0:T(8,128)(2,1)S(1)}, bf16[24,1152]{1,0:T(8,128)(2,1)S(1)}, u32[]{:S(2)}, u32[]{:S(2)}) collective-permute-start(bf16[24,1152]{1,0:T(8,128)(2,1)S(1)} %get-tuple-element.20), channel_id=1, source_target_pairs={{0,384},{48,432},{96,480},{144,528},{192,576},{240,624},{288,672},... | collective-permute-start | bytes 165896 | tf_op jit(solution)/shard_map/ppermute | solution.py:68
  90.1 13.3 %collective-permute-start.7 = (bf16[24,1152]{1,0:T(8,128)(2,1)S(1)}, bf16[24,1152]{1,0:T(8,128)(2,1)S(1)}, u32[]{:S(2)}, u32[]{:S(2)}) collective-permute-start(bf16[24,1152]{1,0:T(8,128)(2,1)S(1)} %get-tuple-element.18), channel_id=1, source_target_pairs={{0,192},{48,240},{96,288},{144,336},{192,0},{240,48},{288,96},{336... | collective-permute-start | bytes 165896 | tf_op jit(solution)/shard_map/ppermute | solution.py:68

commit v5 on v3

--- a/solution.py
+++ b/solution.py
@@ -109,7 +109,7 @@
     gy = (gy_own + gy_got.astype(F32)).reshape(4, 4, ROWS, width)
     gy = scatter_sum(gy)
     gx = jnp.sum(gx.astype(F32), 0)
-    own_images = lax.dynamic_slice_in_dim(images, group * ROWS, ROWS, 0)
+    own_images = lax.optimization_barrier(lax.dynamic_slice_in_dim(images, group * ROWS, ROWS, 0))
     unit_x, inv_x = normalize(own_images)
     unit_y, inv_y = normalize(texts)
     gx = (gx - unit_y.astype(BF).astype(F32)) * scale

time: 104 us -> 105 us (level)
  the two profiles are of different devices: /device:TPU:64 before, /device:TPU:72 now
where the time goes in v5:
time: 105 us
  starting transfers between devices  54.8 us (52%)
  waiting for transfers between devices  29.3 us (28%)
  other arithmetic  9.44 us (9%)
  matrix products  4.84 us (5%)
  local copies, waits for them, and re-layouts  3.72 us (4%)
  between operations  2.4 us (2%)
    ppermute x6, starting transfers between devices, scatter_sum(): lax.ppermute(pick(total, 0, at ^ d).astype(BF), PLANE, [(member(*m), memb...  20.4 us
    all_to_all x1, waiting for transfers between devices, gather(): own = lax.all_to_all(copies, PLANE, 0, 0, axis_index_groups=groups)  15.5 us
    all_to_all x1, starting transfers between devices, local(): gx = lax.all_to_all(gx, ('yh', 'z3'), 0, 0)  12.4 us
    all_to_all x1, waiting for transfers between devices, local(): gx = lax.all_to_all(gx, ('yh', 'z3'), 0, 0)  9.24 us
    all_to_all x1, starting transfers between devices, gather(): own = lax.all_to_all(copies, PLANE, 0, 0, axis_index_groups=groups)  7.8 us
    ppermute x1, starting transfers between devices, local(): lax.ppermute(pick(gx, 0, 1 - z2).astype(BF), ('c', 'z3', 'z2', 'z1'), pai...  5.92 us
    ppermute x1, waiting for transfers between devices, local(): gx_got = lax.ppermute(gx_send, ('c', 'z3', 'z2', 'z1'), pair_perm(12, 1))  4.5 us
    ppermute x2, starting transfers between devices, flip(): return lax.ppermute(value, axis, [(i, i ^ distance) for i in range(size)])  4.22 us
  transfers between devices with their start and end apart: 12, of which 3 were waited for; matrix products, arithmetic and copies ran while one was open for 9% of the time, Pallas kernels for 0%

profile of v5, /device:TPU:72, one launch (start us, length us, event | category | flops | bytes accessed | tf_op | source)
XLA Modules:
  0.0 104.5 jit_solution(11211160707403809444)
XLA Ops:
  0.6 1.9 %broadcast_in_dim.2 = bf16[16,24,1152]{2,1,0:T(8,128)(2,1)} broadcast(bf16[24,1152]{1,0:T(8,128)(2,1)} %param.5), dimensions={1,2} | broadcast | bytes 940032 | tf_op jit(solution)/shard_map/broadcast_in_dim | solution.py:59
  2.5 7.8 %all-to-all-start = ((bf16[16,24,1152]{2,1,0:T(8,128)(2,1)}), bf16[16,24,1152]{2,1,0:T(8,128)(2,1)S(1)}, u32[]{:S(2)}, u32[]{:S(2)}) async-start(bf16[16,24,1152]{2,1,0:T(8,128)(2,1)} %broadcast_in_dim.2), calls=%async_computation | async-start | bytes 1769472 | tf_op jit(solution)/shard_map/all_to_all | solution.py:60
  10.3 0.2 constant_dynamic-slice_fusion.1
  10.5 0.1 copy.11
  10.6 0.1 copy.10
  10.7 0.3 multiply_reduce_fusion
  11.0 0.4 copy-done
  11.4 0.2 copy-done.1
  11.7 0.6 constant_dynamic-slice_fusion.2
  12.3 1.5 %maximum_convert_fusion = f32[24,24,1152]{2,1,0:T(8,128)S(1)} fusion(bf16[12,24,1152]{2,1,0:T(8,128)(2,1)} %bitcast.66, bf16[12,24,1152]{2,1,0:T(8,128)(2,1)} %bitcast.68), kind=kLoop, calls=%fused_computation.12 | loop fusion | flops 1327104 | bytes 3981312 | tf_op jit(solution)/shard_map/convert_element_type | solution.py:14
  13.8 15.5 %all-to-all-done = bf16[16,24,1152]{2,1,0:T(8,128)(2,1)S(1)} async-done(((bf16[16,24,1152]{2,1,0:T(8,128)(2,1)}), bf16[16,24,1152]{2,1,0:T(8,128)(2,1)S(1)}, u32[]{:S(2)}, u32[]{:S(2)}) %all-to-all-start) | async-done | bytes 884768 | tf_op jit(solution)/shard_map/all_to_all | solution.py:60
  29.3 1.9 %collective-permute-start = (bf16[384,1152]{1,0:T(8,128)(2,1)S(1)}, bf16[384,1152]{1,0:T(8,128)(2,1)}, u32[]{:S(2)}, u32[]{:S(2)}) collective-permute-start(bf16[384,1152]{1,0:T(8,128)(2,1)S(1)} %bitcast.62), channel_id=1, source_target_pairs={{0,24},{24,0},{1,25},{25,1},{2,26},{26,2},{3,27},{27,3},{4,28},{28... | collective-permute-start | bytes 2654216 | tf_op jit(solution)/shard_map/ppermute | solution.py:37
  31.2 1.4 %fusion.31 = f32[24]{0:T(128)} fusion(bf16[24,1152]{1,0:T(8,128)(2,1)} %param.5), kind=kLoop, calls=%fused_computation.51 | loop fusion | flops 82920 | bytes 55392 | tf_op jit(solution)/shard_map/reduce_sum | solution.py:15
  33.4 0.1 rsqrt.37
  34.1 0.7 add_rsqrt_fusion.2
  34.8 0.2 fusion.2
  35.0 0.0 collective-permute-done
  35.0 1.6 %fusion = f32[768]{0:T(1024)S(1)} fusion(bf16[384,1152]{1,0:T(8,128)(2,1)} %collective-permute-done, bf16[384,1152]{1,0:T(8,128)(2,1)S(1)} %bitcast.63), kind=kLoop, calls=%fused_computation.2 | loop fusion | flops 5307648 | bytes 1772544 | tf_op jit(solution)/shard_map/reduce_sum | solution.py:15
  36.6 1.5 %fusion.1 = bf16[768,1152]{1,0:T(8,128)(2,1)S(1)} fusion(f32[768]{0:T(1024)S(1)} %add_rsqrt_fusion.1, bf16[384,1152]{1,0:T(8,128)(2,1)} %collective-permute-done, bf16[384,1152]{1,0:T(8,128)(2,1)S(1)} %bitcast.64), kind=kLoop, calls=%fused_computation.3 | loop fusion | flops 5308416 | bytes 3542016 | tf_op jit(solution)/shard_map/convert_element_type | solution.py:91
  38.1 1.5 %divide_convert_fusion = bf16[576,768]{1,0:T(8,128)(2,1)S(1)} fusion(bf16[576,1152]{1,0:T(8,128)(2,1)S(1)} %fusion.2, bf16[768,1152]{1,0:T(8,128)(2,1)S(1)} %fusion.1, f32[]{:T(128)} %bitcast.61, f32[]{:T(128)} %bitcast.9), kind=kOutput, calls=%fused_computation.11 | convolution fusion | flops 1021870080 | bytes 3981320 | tf_op jit(solution)/shard_map/dot_general | solution.py:92
  39.7 0.0 copy-start.3
  39.7 0.7 convolution_convert_fusion.1
  40.4 4.1 %collective-permute-start.1 = (bf16[288,1152]{1,0:T(8,128)(2,1)S(1)}, bf16[288,1152]{1,0:T(8,128)(2,1)S(1)}, u32[]{:S(2)}, u32[]{:S(2)}) collective-permute-start(bf16[288,1152]{1,0:T(8,128)(2,1)S(1)} %convolution_convert_fusion.1), channel_id=1, source_target_pairs={{0,1},{1,0},{2,3},{3,2},{4,5},{5,4},{6,7},{7,6},{8,9},{9,8},{10,11... | collective-permute-start | bytes 1990664 | tf_op jit(solution)/shard_map/ppermute | solution.py:98
  44.5 0.1 fusion.27
  44.7 0.9 convolution_convert_fusion
  45.6 2.3 %collective-permute-start.3 = (bf16[384,1152]{1,0:T(8,128)(2,1)S(1)}, bf16[384,1152]{1,0:T(8,128)(2,1)S(1)}, u32[]{:S(2)}, u32[]{:S(2)}) collective-permute-start(bf16[384,1152]{1,0:T(8,128)(2,1)S(1)} %convolution_convert_fusion), channel_id=1, source_target_pairs={{0,24},{24,0},{1,25},{25,1},{2,26},{26,2},{3,27},{27,3},{4,28},{28... | collective-permute-start | bytes 2654216 | tf_op jit(solution)/shard_map/ppermute | solution.py:37
  47.9 0.7 fusion.12
  48.7 4.5 %collective-permute-done.1 = bf16[288,1152]{1,0:T(8,128)(2,1)S(1)} collective-permute-done((bf16[288,1152]{1,0:T(8,128)(2,1)S(1)}, bf16[288,1152]{1,0:T(8,128)(2,1)S(1)}, u32[]{:S(2)}, u32[]{:S(2)}) %collective-permute-start.1) | collective-permute-done | bytes 663584 | tf_op jit(solution)/shard_map/ppermute | solution.py:98
  53.2 0.1 convert_add_fusion.1
  53.3 5.9 %collective-permute-start.2 = (bf16[6,24,1152]{2,1,0:T(8,128)(2,1)S(1)}, bf16[6,24,1152]{2,1,0:T(8,128)(2,1)S(1)}, u32[]{:S(2)}, u32[]{:S(2)}) collective-permute-start(bf16[6,24,1152]{2,1,0:T(8,128)(2,1)S(1)} %fusion.14), channel_id=1, source_target_pairs={{0,2},{1,3},{2,0},{3,1},{4,6},{5,7},{6,4},{7,5},{8,10},{9,11},{10,... | collective-permute-start | bytes 995336 | tf_op jit(solution)/shard_map/ppermute | solution.py:106
  59.3 0.9 convert_add_fusion
  60.2 0.1 fusion.15
  60.3 2.8 %collective-permute-start.6 = (bf16[4,24,1152]{2,1,0:T(8,128)(2,1)S(1)}, bf16[4,24,1152]{2,1,0:T(8,128)(2,1)S(1)}, u32[]{:S(2)}, u32[]{:S(2)}) collective-permute-start(bf16[4,24,1152]{2,1,0:T(8,128)(2,1)S(1)} %get-tuple-element.14), channel_id=1, source_target_pairs={{0,144},{48,96},{96,48},{144,0},{192,336},{240,288},{288,240},{336... | collective-permute-start | bytes 663560 | tf_op jit(solution)/shard_map/ppermute | solution.py:68
  63.1 2.5 %collective-permute-start.5 = (bf16[4,24,1152]{2,1,0:T(8,128)(2,1)S(1)}, bf16[4,24,1152]{2,1,0:T(8,128)(2,1)S(1)}, u32[]{:S(2)}, u32[]{:S(2)}) collective-permute-start(bf16[4,24,1152]{2,1,0:T(8,128)(2,1)S(1)} %get-tuple-element.15), channel_id=1, source_target_pairs={{0,96},{48,144},{96,0},{144,48},{192,288},{240,336},{288,192},{336... | collective-permute-start | bytes 663560 | tf_op jit(solution)/shard_map/ppermute | solution.py:68
  65.5 4.6 %collective-permute-start.4 = (bf16[4,24,1152]{2,1,0:T(8,128)(2,1)S(1)}, bf16[4,24,1152]{2,1,0:T(8,128)(2,1)S(1)}, u32[]{:S(2)}, u32[]{:S(2)}) collective-permute-start(bf16[4,24,1152]{2,1,0:T(8,128)(2,1)S(1)} %get-tuple-element.13), channel_id=1, source_target_pairs={{0,48},{48,0},{96,144},{144,96},{192,240},{240,192},{288,336},{336... | collective-permute-start | bytes 663560 | tf_op jit(solution)/shard_map/ppermute | solution.py:68
  70.2 0.8 fusion.3
  70.9 12.4 %all-to-all-start.1 = ((bf16[6,24,1152]{2,1,0:T(8,128)(2,1)}), bf16[6,24,1152]{2,1,0:T(8,128)(2,1)S(1)}, u32[]{:S(2)}, u32[]{:S(2)}) async-start(bf16[6,24,1152]{2,1,0:T(8,128)(2,1)} %fusion.3), calls=%async_computation.1 | async-start | bytes 663552 | tf_op jit(solution)/shard_map/all_to_all | solution.py:108
  83.3 0.0 collective-permute-done.6
  83.4 0.0 collective-permute-done.4
  83.4 0.1 fusion.6
  83.5 2.2 %collective-permute-start.9 = (bf16[24,1152]{1,0:T(8,128)(2,1)S(1)}, bf16[24,1152]{1,0:T(8,128)(2,1)S(1)}, u32[]{:S(2)}, u32[]{:S(2)}) collective-permute-start(bf16[24,1152]{1,0:T(8,128)(2,1)S(1)} %get-tuple-element.19), channel_id=1, source_target_pairs={{0,576},{48,624},{96,672},{144,720},{192,384},{240,432},{288,480},... | collective-permute-start | bytes 165896 | tf_op jit(solution)/shard_map/ppermute | solution.py:68
  85.7 5.0 %collective-permute-start.8 = (bf16[24,1152]{1,0:T(8,128)(2,1)S(1)}, bf16[24,1152]{1,0:T(8,128)(2,1)S(1)}, u32[]{:S(2)}, u32[]{:S(2)}) collective-permute-start(bf16[24,1152]{1,0:T(8,128)(2,1)S(1)} %get-tuple-element.20), channel_id=1, source_target_pairs={{0,384},{48,432},{96,480},{144,528},{192,576},{240,624},{288,672},... | collective-permute-start | bytes 165896 | tf_op jit(solution)/shard_map/ppermute | solution.py:68
  90.8 3.4 %collective-permute-start.7 = (bf16[24,1152]{1,0:T(8,128)(2,1)S(1)}, bf16[24,1152]{1,0:T(8,128)(2,1)S(1)}, u32[]{:S(2)}, u32[]{:S(2)}) collective-permute-start(bf16[24,1152]{1,0:T(8,128)(2,1)S(1)} %get-tuple-element.18), channel_id=1, source_target_pairs={{0,192},{48,240},{96,288},{144,336},{192,0},{240,48},{288,96},{336... | collective-permute-start | bytes 165896 | tf_op jit(solution)/shard_map/ppermute | solution.py:68
  94.2 9.2 %all-to-all-done.1 = bf16[6,24,1152]{2,1,0:T(8,128)(2,1)S(1)} async-done(((bf16[6,24,1152]{2,1,0:T(8,128)(2,1)}), bf16[6,24,1152]{2,1,0:T(8,128)(2,1)S(1)}, u32[]{:S(2)}, u32[]{:S(2)}) %all-to-all-start.1) | async-done | bytes 331808 | tf_op jit(solution)/shard_map/all_to_all | solution.py:108
  103.5 0.0 collective-permute-done.8
  103.5 0.0 collective-permute-done.7
  103.5 0.2 fusion.28
  103.7 0.8 fusion.30
  (17 shorter events, 0.2 us)
Async XLA Ops:
  0.6 9.7 %copy-start.2 = (bf16[576,1152]{1,0:T(8,128)(2,1)S(1)}, bf16[576,1152]{1,0:T(8,128)(2,1)}, u32[]{:S(2)}) copy-start(bf16[576,1152]{1,0:T(8,128)(2,1)} %param.4) | copy-start | bytes 3981316
  2.5 26.8 %all-to-all-start = ((bf16[16,24,1152]{2,1,0:T(8,128)(2,1)}), bf16[16,24,1152]{2,1,0:T(8,128)(2,1)S(1)}, u32[]{:S(2)}, u32[]{:S(2)}) async-start(bf16[16,24,1152]{2,1,0:T(8,128)(2,1)} %broadcast_in_dim.2), calls=%async_computation | async-start | bytes 1769472 | tf_op jit(solution)/shard_map/all_to_all | solution.py:60
  10.6 0.9 copy-start
  10.6 1.0 copy-start.1
  29.3 5.7 %collective-permute-start = (bf16[384,1152]{1,0:T(8,128)(2,1)S(1)}, bf16[384,1152]{1,0:T(8,128)(2,1)}, u32[]{:S(2)}, u32[]{:S(2)}) collective-permute-start(bf16[384,1152]{1,0:T(8,128)(2,1)S(1)} %bitcast.62), channel_id=1, source_target_pairs={{0,24},{24,0},{1,25},{25,1},{2,26},{26,2},{3,27},{27,3},{4,28},{28... | collective-permute-start | bytes 2654216 | tf_op jit(solution)/shard_map/ppermute | solution.py:37
  39.7 4.9 %copy-start.3 = (bf16[24,1152]{1,0:T(8,128)(2,1)S(1)}, bf16[24,1152]{1,0:T(8,128)(2,1)}, u32[]{:S(2)}) copy-start(bf16[24,1152]{1,0:T(8,128)(2,1)} %constant_dynamic-slice_fusion.2) | copy-start | bytes 165892
  40.4 12.7 %collective-permute-start.1 = (bf16[288,1152]{1,0:T(8,128)(2,1)S(1)}, bf16[288,1152]{1,0:T(8,128)(2,1)S(1)}, u32[]{:S(2)}, u32[]{:S(2)}) collective-permute-start(bf16[288,1152]{1,0:T(8,128)(2,1)S(1)} %convolution_convert_fusion.1), channel_id=1, source_target_pairs={{0,1},{1,0},{2,3},{3,2},{4,5},{5,4},{6,7},{7,6},{8,9},{9,8},{10,11... | collective-permute-start | bytes 1990664 | tf_op jit(solution)/shard_map/ppermute | solution.py:98
  45.6 13.7 %collective-permute-start.3 = (bf16[384,1152]{1,0:T(8,128)(2,1)S(1)}, bf16[384,1152]{1,0:T(8,128)(2,1)S(1)}, u32[]{:S(2)}, u32[]{:S(2)}) collective-permute-start(bf16[384,1152]{1,0:T(8,128)(2,1)S(1)} %convolution_convert_fusion), channel_id=1, source_target_pairs={{0,24},{24,0},{1,25},{25,1},{2,26},{26,2},{3,27},{27,3},{4,28},{28... | collective-permute-start | bytes 2654216 | tf_op jit(solution)/shard_map/ppermute | solution.py:37
  53.3 16.8 %collective-permute-start.2 = (bf16[6,24,1152]{2,1,0:T(8,128)(2,1)S(1)}, bf16[6,24,1152]{2,1,0:T(8,128)(2,1)S(1)}, u32[]{:S(2)}, u32[]{:S(2)}) collective-permute-start(bf16[6,24,1152]{2,1,0:T(8,128)(2,1)S(1)} %fusion.14), channel_id=1, source_target_pairs={{0,2},{1,3},{2,0},{3,1},{4,6},{5,7},{6,4},{7,5},{8,10},{9,11},{10,... | collective-permute-start | bytes 995336 | tf_op jit(solution)/shard_map/ppermute | solution.py:106
  60.3 23.0 %collective-permute-start.6 = (bf16[4,24,1152]{2,1,0:T(8,128)(2,1)S(1)}, bf16[4,24,1152]{2,1,0:T(8,128)(2,1)S(1)}, u32[]{:S(2)}, u32[]{:S(2)}) collective-permute-start(bf16[4,24,1152]{2,1,0:T(8,128)(2,1)S(1)} %get-tuple-element.14), channel_id=1, source_target_pairs={{0,144},{48,96},{96,48},{144,0},{192,336},{240,288},{288,240},{336... | collective-permute-start | bytes 663560 | tf_op jit(solution)/shard_map/ppermute | solution.py:68
  63.1 20.3 %collective-permute-start.5 = (bf16[4,24,1152]{2,1,0:T(8,128)(2,1)S(1)}, bf16[4,24,1152]{2,1,0:T(8,128)(2,1)S(1)}, u32[]{:S(2)}, u32[]{:S(2)}) collective-permute-start(bf16[4,24,1152]{2,1,0:T(8,128)(2,1)S(1)} %get-tuple-element.15), channel_id=1, source_target_pairs={{0,96},{48,144},{96,0},{144,48},{192,288},{240,336},{288,192},{336... | collective-permute-start | bytes 663560 | tf_op jit(solution)/shard_map/ppermute | solution.py:68
  65.5 17.8 %collective-permute-start.4 = (bf16[4,24,1152]{2,1,0:T(8,128)(2,1)S(1)}, bf16[4,24,1152]{2,1,0:T(8,128)(2,1)S(1)}, u32[]{:S(2)}, u32[]{:S(2)}) collective-permute-start(bf16[4,24,1152]{2,1,0:T(8,128)(2,1)S(1)} %get-tuple-element.13), channel_id=1, source_target_pairs={{0,48},{48,0},{96,144},{144,96},{192,240},{240,192},{288,336},{336... | collective-permute-start | bytes 663560 | tf_op jit(solution)/shard_map/ppermute | solution.py:68
  70.9 32.5 %copy-start.4 = (bf16[24,1152]{1,0:T(8,128)(2,1)S(1)}, bf16[24,1152]{1,0:T(8,128)(2,1)}, u32[]{:S(2)}) copy-start(bf16[24,1152]{1,0:T(8,128)(2,1)} %param.5) | copy-start | bytes 165892
  70.9 32.5 %all-to-all-start.1 = ((bf16[6,24,1152]{2,1,0:T(8,128)(2,1)}), bf16[6,24,1152]{2,1,0:T(8,128)(2,1)S(1)}, u32[]{:S(2)}, u32[]{:S(2)}) async-start(bf16[6,24,1152]{2,1,0:T(8,128)(2,1)} %fusion.3), calls=%async_computation.1 | async-start | bytes 663552 | tf_op jit(solution)/shard_map/all_to_all | solution.py:108
  83.5 19.9 %collective-permute-start.9 = (bf16[24,1152]{1,0:T(8,128)(2,1)S(1)}, bf16[24,1152]{1,0:T(8,128)(2,1)S(1)}, u32[]{:S(2)}, u32[]{:S(2)}) collective-permute-start(bf16[24,1152]{1,0:T(8,128)(2,1)S(1)} %get-tuple-element.19), channel_id=1, source_target_pairs={{0,576},{48,624},{96,672},{144,720},{192,384},{240,432},{288,480},... | collective-permute-start | bytes 165896 | tf_op jit(solution)/shard_map/ppermute | solution.py:68
  85.7 17.7 %collective-permute-start.8 = (bf16[24,1152]{1,0:T(8,128)(2,1)S(1)}, bf16[24,1152]{1,0:T(8,128)(2,1)S(1)}, u32[]{:S(2)}, u32[]{:S(2)}) collective-permute-start(bf16[24,1152]{1,0:T(8,128)(2,1)S(1)} %get-tuple-element.20), channel_id=1, source_target_pairs={{0,384},{48,432},{96,480},{144,528},{192,576},{240,624},{288,672},... | collective-permute-start | bytes 165896 | tf_op jit(solution)/shard_map/ppermute | solution.py:68
  90.8 12.7 %collective-permute-start.7 = (bf16[24,1152]{1,0:T(8,128)(2,1)S(1)}, bf16[24,1152]{1,0:T(8,128)(2,1)S(1)}, u32[]{:S(2)}, u32[]{:S(2)}) collective-permute-start(bf16[24,1152]{1,0:T(8,128)(2,1)S(1)} %get-tuple-element.18), channel_id=1, source_target_pairs={{0,192},{48,240},{96,288},{144,336},{192,0},{240,48},{288,96},{336... | collective-permute-start | bytes 165896 | tf_op jit(solution)/shard_map/ppermute | solution.py:68
